TPU v7x, 512 devices: a whole 4x4x16 slice. The times are simulated.
512 devices in a mesh: ctx: 64 (over y, z), head: 8 (over x, core).
Axes of the slice: x: 4, y: 4, z: 16, core: 2. Of those that a mesh axis runs over, the one named last changes fastest.
Arguments:
- queries: bfloat16 [32768, 4096], P(('ctx', 'head')), may hold values from -0.0029296875 to 0.0029296875
- keys: bfloat16 [32768, 4096], P(('ctx', 'head')), may hold values from -0.0029296875 to 0.0029296875
- values: bfloat16 [32768, 4096], P(('ctx', 'head')), may hold values from -6 to 6
- grad_out: bfloat16 [32768, 4096], P(('ctx', 'head')), may hold values from -6 to 6
Outputs:
- grad_queries: bfloat16 [32768, 4096], P(('ctx', 'head'))
- grad_keys: bfloat16 [32768, 4096], P(('ctx', 'head'))
- grad_values: bfloat16 [32768, 4096], P(('ctx', 'head'))
All inputs are finite; a program needn't handle non-finite values.
Results may differ from a plain program's by a relative error of at most 0.005.
Values may be sent and summed in bfloat16 or wider, within the bound.
No kernel may reach another device: no remote copies, remote signals or barrier semaphores. Data moves between devices by JAX's collectives and lax.ppermute only.
A program may use at most 128 MiB of HBM per device.

v0:
```python
import jax
import jax.numpy as jnp
from jax import lax
from jax.sharding import PartitionSpec as P

HEADS = 32
HEAD_DIM = 128


def carried_in(part, axis, combine, identity, reverse):
    count = lax.axis_size(axis)
    place = lax.axis_index(axis)
    ahead = count - 1 - place if reverse else place
    gathered = lax.all_gather(part, axis)
    state = jnp.zeros_like(part) + jnp.asarray(identity, part.dtype)

    def one(hop, state):
        source = count - 1 - hop if reverse else hop
        return combine(state, lax.dynamic_index_in_dim(gathered, source, 0, False))

    return lax.fori_loop(0, ahead, one, state)


def add_states(earlier, later_part):
    return jax.tree.map(jnp.add, earlier, later_part)


def local(queries, keys, values, grad_out):
    head_count = lax.axis_size("head")
    tok_rows, width = queries.shape
    group_heads = HEADS // head_count

    def to_groups(array):
        return array.reshape(tok_rows, head_count, group_heads * HEAD_DIM)

    query_g, key_g, value_g, grad_g = (
        lax.all_to_all(to_groups(queries), "head", split_axis=1, concat_axis=0, tiled=True),
        lax.all_to_all(to_groups(keys), "head", split_axis=1, concat_axis=0, tiled=True),
        lax.all_to_all(to_groups(values), "head", split_axis=1, concat_axis=0, tiled=True),
        lax.all_to_all(to_groups(grad_out), "head", split_axis=1, concat_axis=0, tiled=True),
    )
    length = query_g.shape[0]
    query_g = query_g.reshape(length, group_heads, HEAD_DIM)
    key_g = key_g.reshape(length, group_heads, HEAD_DIM)
    value_g = value_g.reshape(length, group_heads, HEAD_DIM)
    grad_g = grad_g.reshape(length, group_heads, HEAD_DIM)
    span_state = jnp.einsum("lgi,lgj->gij", key_g, value_g, preferred_element_type=jnp.float32)
    span_adjoint = jnp.einsum("lgi,lgj->gij", query_g, grad_g, preferred_element_type=jnp.float32)
    zero_state = jnp.zeros_like(span_state)
    prior_state = carried_in(span_state, "ctx", add_states, zero_state, False)
    later_adjoint = carried_in(span_adjoint, "ctx", add_states, zero_state, True)
    prior_low = prior_state.astype(jnp.bfloat16)
    later_low = later_adjoint.astype(jnp.bfloat16)
    lower = jnp.arange(length)[:, None] >= jnp.arange(length)[None, :]
    value_scores = jnp.einsum("tgj,sgj->gts", grad_g, value_g, preferred_element_type=jnp.float32)
    value_scores = jnp.where(lower[None], value_scores, 0.0).astype(jnp.bfloat16)
    key_scores = jnp.einsum("tgi,sgi->gts", query_g, key_g, preferred_element_type=jnp.float32)
    key_scores = jnp.where(lower[None], key_scores, 0.0).astype(jnp.bfloat16)
    grad_query = jnp.einsum(
        "gts,sgi->tgi", value_scores, key_g, preferred_element_type=jnp.float32
    ) + jnp.einsum("tgj,gij->tgi", grad_g, prior_low, preferred_element_type=jnp.float32)
    grad_key = jnp.einsum(
        "gts,tgi->sgi", value_scores, query_g, preferred_element_type=jnp.float32
    ) + jnp.einsum("sgj,gij->sgi", value_g, later_low, preferred_element_type=jnp.float32)
    grad_value = jnp.einsum(
        "gts,tgj->sgj", key_scores, grad_g, preferred_element_type=jnp.float32
    ) + jnp.einsum("sgi,gij->sgj", key_g, later_low, preferred_element_type=jnp.float32)

    def to_send(array):
        return array.astype(jnp.bfloat16).reshape(length, 1, group_heads * HEAD_DIM)

    back_query, back_key, back_value = (
        lax.all_to_all(to_send(grad_query), "head", split_axis=0, concat_axis=1, tiled=True),
        lax.all_to_all(to_send(grad_key), "head", split_axis=0, concat_axis=1, tiled=True),
        lax.all_to_all(to_send(grad_value), "head", split_axis=0, concat_axis=1, tiled=True),
    )
    return (
        back_query.reshape(tok_rows, width),
        back_key.reshape(tok_rows, width),
        back_value.reshape(tok_rows, width),
    )


def solution(mesh):
    return jax.shard_map(
        local,
        mesh=mesh,
        in_specs=(
            P(("ctx", "head"), None),
            P(("ctx", "head"), None),
            P(("ctx", "head"), None),
            P(("ctx", "head"), None),
        ),
        out_specs=(P(("ctx", "head"), None), P(("ctx", "head"), None), P(("ctx", "head"), None)),
        check_vma=False,
    )
```

profile of v0, /device:TPU:504, one launch (start us, length us, event | category | flops | bytes accessed | tf_op | source)
XLA Modules:
  0.0 509.0 jit_solution(8912885961342150516)
XLA Ops:
  7.2 1.9 copy.125
  9.1 4.4 all-to-all-start.4
  13.5 1.9 copy.128
  15.4 8.5 %all-to-all-done.4 = bf16[64,8,512]{2,0,1:T(8,128)(2,1)S(1)} async-done(((bf16[64,8,512]{2,0,1:T(8,128)(2,1)}), bf16[64,8,512]{2,0,1:T(8,128)(2,1)S(1)}, u32[]{:S(2)}, u32[]{:S(2)}) %all-to-all-start.4) | async-done | bytes 524320 | tf_op jit(solution)/shard_map/all_to_all | solution.py:37
  23.8 3.5 all-to-all-start
  27.5 10.1 %all-to-all-done = bf16[64,8,512]{2,0,1:T(8,128)(2,1)S(1)} async-done(((bf16[64,8,512]{2,0,1:T(8,128)(2,1)}), bf16[64,8,512]{2,0,1:T(8,128)(2,1)S(1)}, u32[]{:S(2)}, u32[]{:S(2)}) %all-to-all-start) | async-done | bytes 524320 | tf_op jit(solution)/shard_map/all_to_all | solution.py:40
  40.0 3.5 all-to-all-start.2
  44.3 9.4 %all-to-all-done.2 = bf16[64,8,512]{2,0,1:T(8,128)(2,1)S(1)} async-done(((bf16[64,8,512]{2,0,1:T(8,128)(2,1)}), bf16[64,8,512]{2,0,1:T(8,128)(2,1)S(1)}, u32[]{:S(2)}, u32[]{:S(2)}) %all-to-all-start.2) | async-done | bytes 524320 | tf_op jit(solution)/shard_map/all_to_all | solution.py:38
  53.8 3.5 all-to-all-start.1
  57.5 10.1 %all-to-all-done.1 = bf16[64,8,512]{2,0,1:T(8,128)(2,1)S(1)} async-done(((bf16[64,8,512]{2,0,1:T(8,128)(2,1)}), bf16[64,8,512]{2,0,1:T(8,128)(2,1)S(1)}, u32[]{:S(2)}, u32[]{:S(2)}) %all-to-all-start.1) | async-done | bytes 524320 | tf_op jit(solution)/shard_map/all_to_all | solution.py:39
  69.6 2.1 select_convert_fusion.1
  73.1 152.3 %all-gather.7.cloned.1.call-done = f32[256,128,128]{2,1,0:T(8,128)} async-done(((f32[4,128,128]{2,1,0:T(8,128)}), f32[256,128,128]{2,1,0:T(8,128)}) %all-gather.7.cloned.1.call-update) | async-done | bytes 16777232 | tf_op jit(solution)/shard_map/all_gather | solution.py:14
  226.8 3.3 fusion.5
  230.7 2.1 reduce.2
  233.7 2.3 reshape.87
  236.0 4.3 all-to-all-start.6
  240.3 1.8 convolution_bitcast_fusion.1
  245.0 5.8 %all-to-all-done.6 = bf16[8,2,16384]{2,1,0:T(2,128)(2,1)} async-done(((bf16[8,2,16384]{2,1,0:T(2,128)(2,1)}), bf16[8,2,16384]{2,1,0:T(2,128)(2,1)}, u32[]{:S(2)}, u32[]{:S(2)}) %all-to-all-start.6) | async-done | bytes 524320 | tf_op jit(solution)/shard_map/all_to_all | solution.py:75
  250.7 3.5 all-to-all-start.5
  254.2 164.0 %all-gather.5.cloned.1.call-done = f32[256,128,128]{2,1,0:T(8,128)} async-done(((f32[4,128,128]{2,1,0:T(8,128)}), f32[256,128,128]{2,1,0:T(8,128)}) %all-gather.5.cloned.1.call-update) | async-done | bytes 16777232 | tf_op jit(solution)/shard_map/all_gather | solution.py:14
  418.3 65.1 %while.22 = (s32[]{:T(128)}, f32[4,128,128]{2,1,0:T(8,128)S(1)}, s32[]{:T(128)}, f32[64,4,128,128]{3,2,1,0:T(8,128)}, s32[]{:T(128)}, /*index=5*/s32[]{:T(128)}, s32[]{:T(128)}) while((s32[]{:T(128)}, f32[4,128,128]{2,1,0:T(8,128)S(1)}, s32[]{:T(128)}, f32[64,4,128,128]{3,2,1,0:T(8,128)}, s32[]{:T(128)}, /*index=5*/s32[]{:T(128)}, ...), condition=%wide.region_1.2_spmd, body=%wide.region_0.1_spmd.sunk | while | flops 65541 | bytes 786555 | solution.py:21
  486.1 4.3 all-to-all-start.3
  490.3 2.2 reshape.88
  495.1 5.6 %all-to-all-done.3 = bf16[8,2,16384]{2,1,0:T(2,128)(2,1)S(1)} async-done(((bf16[8,2,16384]{2,1,0:T(2,128)(2,1)}), bf16[8,2,16384]{2,1,0:T(2,128)(2,1)S(1)}, u32[]{:S(2)}, u32[]{:S(2)}) %all-to-all-start.3) | async-done | bytes 524320 | tf_op jit(solution)/shard_map/all_to_all | solution.py:73
  (119 shorter events, 83.1 us)
Async XLA Ops:
  9.0 30.1 %copy-start.6 = (bf16[64,4096]{1,0:T(8,128)(2,1)S(1)}, bf16[64,4096]{1,0:T(8,128)(2,1)}, u32[]{:S(2)}) copy-start(bf16[64,4096]{1,0:T(8,128)(2,1)} %param.9) | copy-start | bytes 1572868
  9.1 14.8 %all-to-all-start.4 = ((bf16[64,8,512]{2,0,1:T(8,128)(2,1)}), bf16[64,8,512]{2,0,1:T(8,128)(2,1)S(1)}, u32[]{:S(2)}, u32[]{:S(2)}) async-start(bf16[64,8,512]{2,0,1:T(8,128)(2,1)} %bitcast.106), calls=%async_computation.4 | async-start | bytes 1048576 | tf_op jit(solution)/shard_map/all_to_all | solution.py:37
  15.4 28.1 %copy-start.7 = (bf16[64,4096]{1,0:T(8,128)(2,1)S(1)}, bf16[64,4096]{1,0:T(8,128)(2,1)}, u32[]{:S(2)}) copy-start(bf16[64,4096]{1,0:T(8,128)(2,1)} %param.10) | copy-start | bytes 1572868
  23.8 13.8 %all-to-all-start = ((bf16[64,8,512]{2,0,1:T(8,128)(2,1)}), bf16[64,8,512]{2,0,1:T(8,128)(2,1)S(1)}, u32[]{:S(2)}, u32[]{:S(2)}) async-start(bf16[64,8,512]{2,0,1:T(8,128)(2,1)} %bitcast.109), calls=%async_computation | async-start | bytes 1048576 | tf_op jit(solution)/shard_map/all_to_all | solution.py:40
  27.3 198.1 %all-gather.7.cloned.1.call-start = ((), (), s32[]{:S(2)}) async-start(), calls=%async_computation.8 | async-start | bytes 17039360 | tf_op jit(solution)/shard_map/all_gather | solution.py:14
  38.1 19.3 %copy-start = (bf16[512,4,128]{0,2,1:T(8,128)(2,1)}, bf16[512,4,128]{0,2,1:T(8,128)(2,1)S(1)}, u32[]{:S(2)}) copy-start(bf16[512,4,128]{0,2,1:T(8,128)(2,1)S(1)} %copy.80) | copy-start | bytes 1572868
  40.0 13.8 %all-to-all-start.2 = ((bf16[64,8,512]{2,0,1:T(8,128)(2,1)}), bf16[64,8,512]{2,0,1:T(8,128)(2,1)S(1)}, u32[]{:S(2)}, u32[]{:S(2)}) async-start(bf16[64,8,512]{2,0,1:T(8,128)(2,1)} %bitcast.107), calls=%async_computation.2 | async-start | bytes 1048576 | tf_op jit(solution)/shard_map/all_to_all | solution.py:38
  53.8 13.8 %all-to-all-start.1 = ((bf16[64,8,512]{2,0,1:T(8,128)(2,1)}), bf16[64,8,512]{2,0,1:T(8,128)(2,1)S(1)}, u32[]{:S(2)}, u32[]{:S(2)}) async-start(bf16[64,8,512]{2,0,1:T(8,128)(2,1)} %bitcast.108), calls=%async_computation.1 | async-start | bytes 1048576 | tf_op jit(solution)/shard_map/all_to_all | solution.py:39
  57.3 361.0 %all-gather.5.cloned.1.call-start = ((), (), s32[]{:S(2)}) async-start(), calls=%async_computation.7 | async-start | bytes 17039360 | tf_op jit(solution)/shard_map/all_gather | solution.py:14
  67.7 1.1 copy-start.4
  68.9 0.7 copy-start.8
  233.7 8.4 %copy-start.5 = (bf16[512,4,128]{2,1,0:T(4,128)(2,1)S(1)}, bf16[512,4,128]{2,1,0:T(4,128)(2,1)}, u32[]{:S(2)}) copy-start(bf16[512,4,128]{2,1,0:T(4,128)(2,1)} %copy-done.4) | copy-start | bytes 1572868
  236.0 14.7 %all-to-all-start.6 = ((bf16[8,2,16384]{2,1,0:T(2,128)(2,1)}), bf16[8,2,16384]{2,1,0:T(2,128)(2,1)}, u32[]{:S(2)}, u32[]{:S(2)}) async-start(bf16[8,2,16384]{2,1,0:T(2,128)(2,1)} %reshape.87), calls=%async_computation.6 | async-start | bytes 1048576 | tf_op jit(solution)/shard_map/all_to_all | solution.py:75
  240.3 1.8 copy-start.2
  242.4 240.9 %copy-start.1 = (bf16[512,4,128]{0,2,1:T(8,128)(2,1)S(1)}, bf16[512,4,128]{0,2,1:T(8,128)(2,1)}, u32[]{:S(2)}) copy-start(bf16[512,4,128]{0,2,1:T(8,128)(2,1)} %copy-done) | copy-start | bytes 1572868
  242.4 240.9 %copy-start.3 = (f32[512,4,128]{0,2,1:T(8,128)S(1)}, f32[512,4,128]{0,2,1:T(8,128)}, u32[]{:S(2)}) copy-start(f32[512,4,128]{0,2,1:T(8,128)} %convolution_bitcast_fusion.1) | copy-start | bytes 3145732
  250.7 235.3 %all-to-all-start.5 = ((bf16[8,2,16384]{2,1,0:T(2,128)(2,1)}), bf16[8,2,16384]{2,1,0:T(2,128)(2,1)S(1)}, u32[]{:S(2)}, u32[]{:S(2)}) async-start(bf16[8,2,16384]{2,1,0:T(2,128)(2,1)} %reshape.85), calls=%async_computation.5 | async-start | bytes 1048576 | tf_op jit(solution)/shard_map/all_to_all | solution.py:74
  486.1 14.6 %all-to-all-start.3 = ((bf16[8,2,16384]{2,1,0:T(2,128)(2,1)}), bf16[8,2,16384]{2,1,0:T(2,128)(2,1)S(1)}, u32[]{:S(2)}, u32[]{:S(2)}) async-start(bf16[8,2,16384]{2,1,0:T(2,128)(2,1)} %reshape.83), calls=%async_computation.3 | async-start | bytes 1048576 | tf_op jit(solution)/shard_map/all_to_all | solution.py:73
Sparse Core Ops, SparseCore 0:
  39.3 186.0 all-gather.6
  228.3 189.8 all-gather.4
where the time goes:
time: 512 us; the launch traced here: 509 us
  waiting for transfers between devices  366 us (71%)
  other arithmetic  67.9 us (13%)
  starting transfers between devices  27 us (5%)
  local copies, waits for them, and re-layouts  19.8 us (4%)
  between operations  14.3 us (3%)
  matrix products  12.8 us (2%)
    all_gather x2, waiting for transfers between devices, carried_in(): gathered = lax.all_gather(part, axis)  316 us
    add x63, other arithmetic, add_states(): return jax.tree.map(jnp.add, earlier, later_part)  63.7 us
    unnamed x33, local copies, waits for them, and re-layouts  12.9 us
  transfers between devices with their start and end apart: 9, of which 8 were waited for; matrix products, arithmetic and copies ran while one was open for 19% of the time, Pallas kernels for 0%

commit v1 on v0

v1 whole, which is shorter than its diff:
```python
import functools

import jax
import jax.numpy as jnp
from jax import lax
from jax.experimental import pallas as pl
from jax.experimental.pallas import tpu as pltpu
from jax.sharding import Mesh
from jax.sharding import PartitionSpec as P

HEADS = 32
HEAD_DIM = 128
CORES, NEAR, FAR = 2, 8, 32
HALF_HEADS = HEADS // CORES
OWNED = HALF_HEADS // NEAR
STEPS = 4
STEP_HEADS = HALF_HEADS // STEPS
F32, BF16 = jnp.float32, jnp.bfloat16
VMEM_LIMIT = 40 * 1024 * 1024


def params(**kwargs):
    return pltpu.CompilerParams(vmem_limit_bytes=VMEM_LIMIT, **kwargs)


def dot(a, b, contract):
    return lax.dot_general(a, b, (((contract[0],), (contract[1],)), ((), ())), preferred_element_type=F32)


def pick_kernel(core_ref, q_ref, k_ref, v_ref, g_ref, out_ref, sems):
    half = out_ref.shape[2]
    first = pl.multiple_of((1 - core_ref[0]) * half, half)
    copies = [
        pltpu.make_async_copy(ref.at[:, pl.ds(first, half)], out_ref.at[i], sems.at[i])
        for i, ref in enumerate((q_ref, k_ref, v_ref, g_ref))
    ]
    for copy in copies:
        copy.start()
    for copy in copies:
        copy.wait()


def pick(core, arrays):
    rows, width = arrays[0].shape
    any_space = pl.BlockSpec(memory_space=pl.ANY)
    return pl.pallas_call(
        pick_kernel,
        out_shape=jax.ShapeDtypeStruct((4, rows, width // CORES), BF16),
        in_specs=[pl.BlockSpec(memory_space=pltpu.SMEM)] + [any_space] * 4,
        out_specs=any_space,
        scratch_shapes=[pltpu.SemaphoreType.DMA((4,))],
        compiler_params=params(),
        name="pick_half",
    )(core, *arrays)


def tokens_of(refs, other_ref, head):
    columns = slice(head * HEAD_DIM, (head + 1) * HEAD_DIM)
    return [
        jnp.concatenate([ref[:, columns], other_ref[i, :, columns]], axis=0) for i, ref in enumerate(refs)
    ]


def state_kernel(core_ref, q_ref, k_ref, v_ref, g_ref, other_ref, out_ref):
    for head in range(STEP_HEADS):
        query, key, value, grad = tokens_of((q_ref, k_ref, v_ref, g_ref), other_ref, head)
        out_ref[head // OWNED, 0, head % OWNED] = dot(key, value, (0, 0)).astype(BF16)
        out_ref[head // OWNED, 1, head % OWNED] = dot(query, grad, (0, 0)).astype(BF16)


def token_specs(rows):
    columns = STEP_HEADS * HEAD_DIM
    own = pl.BlockSpec((rows, columns), lambda i, core: (0, core[0] * STEPS + i))
    other = pl.BlockSpec((4, rows, columns), lambda i, core: (0, 0, i))
    state = pl.BlockSpec((STEP_HEADS // OWNED, 2, OWNED, HEAD_DIM, HEAD_DIM), lambda i, core: (i, 0, 0, 0, 0))
    return own, other, state


def chunk_states(core, arrays, other):
    rows = arrays[0].shape[0]
    own_spec, other_spec, state_spec = token_specs(rows)
    return pl.pallas_call(
        state_kernel,
        out_shape=jax.ShapeDtypeStruct((NEAR, 2, OWNED, HEAD_DIM, HEAD_DIM), BF16),
        grid_spec=pltpu.PrefetchScalarGridSpec(
            num_scalar_prefetch=1,
            grid=(STEPS,),
            in_specs=[own_spec] * 4 + [other_spec],
            out_specs=state_spec,
        ),
        compiler_params=params(),
        name="chunk_states",
    )(core, *arrays, other)


def total_kernel(near_ref, out_ref):
    total = near_ref[0].astype(F32)
    for chip in range(1, NEAR):
        total += near_ref[chip].astype(F32)
    out_ref[...] = total.astype(BF16)


def group_total(near):
    return pl.pallas_call(
        total_kernel,
        out_shape=jax.ShapeDtypeStruct(near.shape[1:], BF16),
        compiler_params=params(),
        name="group_total",
    )(near)


def carry_kernel(place_ref, far_ref, out_ref):
    @pl.when(place_ref[0] < FAR // 2)
    def _():
        total = jnp.zeros(far_ref.shape[1:], F32)
        for group in range(FAR):
            out_ref[group] = total.astype(BF16)
            total += far_ref[group].astype(F32)

    @pl.when(place_ref[0] >= FAR // 2)
    def _():
        total = jnp.zeros(far_ref.shape[1:], F32)
        for group in reversed(range(FAR)):
            out_ref[group] = total.astype(BF16)
            total += far_ref[group].astype(F32)


def group_carry(place, far):
    return pl.pallas_call(
        carry_kernel,
        out_shape=jax.ShapeDtypeStruct(far.shape, BF16),
        in_specs=[pl.BlockSpec(memory_space=pltpu.SMEM), pl.BlockSpec(memory_space=pltpu.VMEM)],
        out_specs=pl.BlockSpec(memory_space=pltpu.VMEM),
        compiler_params=params(),
        name="group_carry",
    )(place, far)


def spread_kernel(near_ref, carry_ref, out_ref):
    for head in range(OWNED):
        total = carry_ref[0, head].astype(F32)
        for chip in range(NEAR):
            out_ref[chip, 0, head] = total.astype(BF16)
            total += near_ref[chip, 0, head].astype(F32)
        total = carry_ref[1, head].astype(F32)
        for chip in reversed(range(NEAR)):
            out_ref[chip, 1, head] = total.astype(BF16)
            total += near_ref[chip, 1, head].astype(F32)


def chip_carry(near, carry):
    return pl.pallas_call(
        spread_kernel,
        out_shape=jax.ShapeDtypeStruct(near.shape, BF16),
        compiler_params=params(),
        name="chip_carry",
    )(near, carry)


def grad_kernel(core_ref, q_ref, k_ref, v_ref, g_ref, other_ref, carry_ref, gq_ref, gk_ref, gv_ref, send_ref):
    rows = q_ref.shape[0]
    core = core_ref[0]

    def place(axis):
        at = lax.broadcasted_iota(jnp.int32, (2 * rows, 2 * rows), axis)
        return jnp.where(at < rows, at + core * rows, at - core * rows)

    lower = place(0) >= place(1)
    for head in range(STEP_HEADS):
        query, key, value, grad = tokens_of((q_ref, k_ref, v_ref, g_ref), other_ref, head)
        prior = carry_ref[head // OWNED, 0, head % OWNED]
        later = carry_ref[head // OWNED, 1, head % OWNED]
        value_scores = jnp.where(lower, dot(grad, value, (1, 1)), 0.0).astype(BF16)
        key_scores = jnp.where(lower, dot(query, key, (1, 1)), 0.0).astype(BF16)
        grads = (
            dot(value_scores, key, (1, 0)) + dot(grad, prior, (1, 1)),
            dot(value_scores, query, (0, 0)) + dot(value, later, (1, 1)),
            dot(key_scores, grad, (0, 0)) + dot(key, later, (1, 0)),
        )
        columns = slice(head * HEAD_DIM, (head + 1) * HEAD_DIM)
        for i, (out_ref, result) in enumerate(zip((gq_ref, gk_ref, gv_ref), grads)):
            result = result.astype(BF16)
            out_ref[:, columns] = result[:rows]
            send_ref[i, :, columns] = result[rows:]


def gradients(core, arrays, other, carry):
    rows, width = arrays[0].shape
    own_spec, other_spec, state_spec = token_specs(rows)
    columns = STEP_HEADS * HEAD_DIM
    return pl.pallas_call(
        grad_kernel,
        out_shape=[jax.ShapeDtypeStruct((rows, width), BF16)] * 3
        + [jax.ShapeDtypeStruct((3, rows, width // CORES), BF16)],
        grid_spec=pltpu.PrefetchScalarGridSpec(
            num_scalar_prefetch=1,
            grid=(STEPS,),
            in_specs=[own_spec] * 4 + [other_spec, state_spec],
            out_specs=[own_spec] * 3 + [pl.BlockSpec((3, rows, columns), lambda i, core: (0, 0, i))],
        ),
        compiler_params=params(),
        name="gradients",
    )(core, *arrays, other, carry)


def place_kernel(core_ref, got_ref, q_in, k_in, v_in, gq_ref, gk_ref, gv_ref, sems):
    half = got_ref.shape[2]
    first = pl.multiple_of((1 - core_ref[0]) * half, half)
    copies = [
        pltpu.make_async_copy(got_ref.at[i], ref.at[:, pl.ds(first, half)], sems.at[i])
        for i, ref in enumerate((gq_ref, gk_ref, gv_ref))
    ]
    for copy in copies:
        copy.start()
    for copy in copies:
        copy.wait()


def place_half(core, got, grads):
    any_space = pl.BlockSpec(memory_space=pl.ANY)
    return pl.pallas_call(
        place_kernel,
        out_shape=[jax.ShapeDtypeStruct(array.shape, array.dtype) for array in grads],
        in_specs=[pl.BlockSpec(memory_space=pltpu.SMEM)] + [any_space] * 4,
        out_specs=[any_space] * 3,
        scratch_shapes=[pltpu.SemaphoreType.DMA((3,))],
        input_output_aliases={2: 0, 3: 1, 4: 2},
        compiler_params=params(),
        name="place_half",
    )(core, got, *grads)


def exchange(array, axes):
    return lax.all_to_all(array, axes, split_axis=0, concat_axis=0, tiled=True)


def local(queries, keys, values, grad_out):
    arrays = (queries, keys, values, grad_out)
    near_axes, far_axes = ("zl", "x"), ("y", "zh")
    swap = [(0, 1), (1, 0)]
    core = lax.axis_index("core").reshape(1)
    place = lax.axis_index(far_axes).reshape(1)
    other = lax.ppermute(pick(core, arrays), "core", swap)
    near = exchange(chunk_states(core, arrays, other), near_axes)
    total = group_total(near)
    far = exchange(total.reshape(FAR, -1, HEAD_DIM), far_axes)
    carry = exchange(group_carry(place, far), far_axes).reshape(total.shape)
    carry = exchange(chip_carry(near, carry), near_axes)
    *grads, send = gradients(core, arrays, other, carry)
    return tuple(place_half(core, lax.ppermute(send, "core", swap), grads))


def solution(mesh):
    devices = mesh.devices.reshape(4, 8, 2, 4, 2)
    chips = Mesh(devices, ("y", "zh", "zl", "x", "core"))
    rows = P(("y", "zh", "zl", "x", "core"), None)
    return jax.shard_map(
        local, mesh=chips, in_specs=(rows,) * 4, out_specs=(rows,) * 3, check_vma=False
    )
```

time: 512 us -> 114 us (0.22)
  the two profiles are of different devices: /device:TPU:504 before, /device:TPU:1 now
where the time goes in v1:
time: 114 us; the launch traced here: 113 us
  blocking collectives  51.3 us (45%)
  starting transfers between devices  30.4 us (27%)
  waiting for transfers between devices  18.1 us (16%)
  Pallas kernels  8.7 us (8%)
  local copies, waits for them, and re-layouts  4.19 us (4%)
    all_to_all x3, blocking collectives, exchange(): return lax.all_to_all(array, axes, split_axis=0, concat_axis=0, tiled=True)  51.3 us
    all_to_all x1, starting transfers between devices, exchange(): return lax.all_to_all(array, axes, split_axis=0, concat_axis=0, tiled=True)  14.3 us
    all_to_all x1, waiting for transfers between devices, exchange(): return lax.all_to_all(array, axes, split_axis=0, concat_axis=0, tiled=True)  14 us
    ppermute x1, starting transfers between devices, local(): other = lax.ppermute(pick(core, arrays), 'core', swap)  8.79 us
    ppermute x1, starting transfers between devices, local(): return tuple(place_half(core, lax.ppermute(send, 'core', swap), grads))  7.36 us
    pallas_call x1, Pallas kernels, gradients(): pl.pallas_call(grad_kernel, out_shape=[jax.ShapeDtypeStruct((rows, width)...  5.29 us
    unnamed x16, local copies, waits for them, and re-layouts  4.19 us
  transfers between devices with their start and end apart: 3, of which 3 were waited for; matrix products, arithmetic and copies ran while one was open for 0% of the time, Pallas kernels for 0%

profile of v1, /device:TPU:1, one launch (start us, length us, event | category | flops | bytes accessed | tf_op | source)
XLA Modules:
  0.0 113.5 jit_solution(17029863132176686890)
XLA Ops:
  0.6 0.0 copy-start
  0.6 1.0 copy-done
  1.7 1.0 copy-done.2
  2.7 1.0 copy-done.4
  3.8 1.0 copy-done.6
  4.8 0.1 pick_half.1
  4.9 8.8 %collective-permute-start = (bf16[4,64,2048]{2,1,0:T(8,128)(2,1)S(1)}, bf16[4,64,2048]{2,1,0:T(8,128)(2,1)S(1)}, u32[]{:S(2)}, u32[]{:S(2)}) collective-permute-start(bf16[4,64,2048]{2,1,0:T(8,128)(2,1)S(1)} %pick_half.1), channel_id=1, source_target_pairs={{0,1},{1,0},{2,3},{3,2},{4,5},{5,4},{6,7},{7,6},{8,9},{9,8},{10,11... | collective-permute-start | bytes 3145736 | tf_op jit(solution)/shard_map/ppermute | solution.py:243
  13.7 2.3 %collective-permute-done.other_ref = bf16[4,64,2048]{2,1,0:T(8,128)(2,1)S(1)} collective-permute-done((bf16[4,64,2048]{2,1,0:T(8,128)(2,1)S(1)}, bf16[4,64,2048]{2,1,0:T(8,128)(2,1)S(1)}, u32[]{:S(2)}, u32[]{:S(2)}) %collective-permute-start) | collective-permute-done | bytes 1048608 | tf_op jit(solution)/shard_map/ppermute | solution.py:243
  16.0 1.4 %chunk_states.1 = bf16[8,2,2,128,128]{4,3,2,1,0:T(8,128)(2,1)S(1)} custom-call(s32[1]{0:T(128)} %bitcast.core_ref, bf16[64,4096]{1,0:T(8,128)(2,1)S(1)} %copy-done, bf16[64,4096]{1,0:T(8,128)(2,1)S(1)} %copy-done.2, bf16[64,4096]{1,0:T(8,128)(2,1)S(1)} %copy-done.4, bf16[64,4096]{1,0:T(8,128)(2,1)S(1)} %copy-done.6, ...), custom_call_target="tpu_custom_call" | custom-call | tf_op jit(solution)/shard_map/chunk_states/pallas_call | solution.py:82
  17.4 16.9 %all_to_all.20.near_ref = bf16[8,2,2,128,128]{4,3,2,1,0:T(8,128)(2,1)S(1)} all-to-all(bf16[8,2,2,128,128]{4,3,2,1,0:T(8,128)(2,1)S(1)} %chunk_states.1), channel_id=1, replica_groups=mesh['y'=4,'zh'=8,'zl'=2,'x'=4,'core'=2] {'zl','x'}, dimensions={0} | all-to-all | bytes 2097152 | tf_op jit(solution)/shard_map/all_to_all | solution.py:234
  34.3 0.8 group_total.1
  35.1 14.3 %all-to-all-start.1 = ((bf16[32,16,128]{2,1,0:T(8,128)(2,1)}), bf16[32,16,128]{2,1,0:T(8,128)(2,1)S(1)}, u32[]{:S(2)}, u32[]{:S(2)}) async-start(bf16[32,16,128]{2,1,0:T(8,128)(2,1)} %bitcast.2), calls=%async_computation.1 | async-start | bytes 262144 | tf_op jit(solution)/shard_map/all_to_all | solution.py:234
  49.4 14.0 %all-to-all-done.1.far_ref = bf16[32,16,128]{2,1,0:T(8,128)(2,1)S(1)} async-done(((bf16[32,16,128]{2,1,0:T(8,128)(2,1)}), bf16[32,16,128]{2,1,0:T(8,128)(2,1)S(1)}, u32[]{:S(2)}, u32[]{:S(2)}) %all-to-all-start.1) | async-done | bytes 131104 | tf_op jit(solution)/shard_map/all_to_all | solution.py:234
  63.4 19.5 %all_to_all.21 = bf16[32,16,128]{2,1,0:T(8,128)(2,1)S(1)} all-to-all(bf16[32,16,128]{2,1,0:T(8,128)(2,1)S(1)} %group_carry.1), channel_id=1, replica_groups=mesh['y'=4,'zh'=8,'zl'=2,'x'=4,'core'=2] {'y','zh'}, dimensions={0} | all-to-all | bytes 262144 | tf_op jit(solution)/shard_map/all_to_all | solution.py:234
  82.9 0.2 chip_carry.1
  83.0 0.0 copy-start.1
  83.0 0.0 copy-start.3
  83.1 0.0 copy-start.5
  83.1 0.0 copy-start.7
  83.1 14.9 %all_to_all.22.carry_ref = bf16[8,2,2,128,128]{4,3,2,1,0:T(8,128)(2,1)S(1)} all-to-all(bf16[8,2,2,128,128]{4,3,2,1,0:T(8,128)(2,1)S(1)} %chip_carry.1), channel_id=1, replica_groups=mesh['y'=4,'zh'=8,'zl'=2,'x'=4,'core'=2] {'zl','x'}, dimensions={0} | all-to-all | bytes 2097152 | tf_op jit(solution)/shard_map/all_to_all | solution.py:234
  98.0 5.3 %gradients.1 = (bf16[64,4096]{1,0:T(8,128)(2,1)}, bf16[64,4096]{1,0:T(8,128)(2,1)}, bf16[64,4096]{1,0:T(8,128)(2,1)}, bf16[3,64,2048]{2,1,0:T(8,128)(2,1)S(1)}) custom-call(s32[1]{0:T(128)} %bitcast.core_ref, bf16[64,4096]{1,0:T(8,128)(2,1)S(1)} %copy-done.1, bf16[64,4096]{1,0:T(8,128)(2,1)S(1)} %copy-done.3, bf16[64,4096]{1,0:T(8,128)(2,1)S(1)} %copy-done.5, ...), custom_call_target="tpu_custom_call" | custom-call | tf_op jit(solution)/shard_map/gradients/pallas_call | solution.py:191
  103.3 7.4 %collective-permute-start.1 = (bf16[3,64,2048]{2,1,0:T(8,128)(2,1)S(1)}, bf16[3,64,2048]{2,1,0:T(8,128)(2,1)S(1)}, u32[]{:S(2)}, u32[]{:S(2)}) collective-permute-start(bf16[3,64,2048]{2,1,0:T(8,128)(2,1)S(1)} %get-tuple-element.7), channel_id=1, source_target_pairs={{0,1},{1,0},{2,3},{3,2},{4,5},{5,4},{6,7},{7,6},{8,9},{9,8},{10,11... | collective-permute-start | bytes 2359304 | tf_op jit(solution)/shard_map/ppermute | solution.py:250
  110.7 1.9 %collective-permute-done.1.got_ref = bf16[3,64,2048]{2,1,0:T(8,128)(2,1)S(1)} collective-permute-done((bf16[3,64,2048]{2,1,0:T(8,128)(2,1)S(1)}, bf16[3,64,2048]{2,1,0:T(8,128)(2,1)S(1)}, u32[]{:S(2)}, u32[]{:S(2)}) %collective-permute-start.1) | collective-permute-done | bytes 786464 | tf_op jit(solution)/shard_map/ppermute | solution.py:250
  112.6 0.9 place_half.1
  (8 shorter events, 0.0 us)
Async XLA Ops:
  0.6 1.0 copy-start
  1.7 1.0 copy-start.2
  2.7 1.0 copy-start.4
  3.8 1.0 copy-start.6
  4.9 11.1 %collective-permute-start = (bf16[4,64,2048]{2,1,0:T(8,128)(2,1)S(1)}, bf16[4,64,2048]{2,1,0:T(8,128)(2,1)S(1)}, u32[]{:S(2)}, u32[]{:S(2)}) collective-permute-start(bf16[4,64,2048]{2,1,0:T(8,128)(2,1)S(1)} %pick_half.1), channel_id=1, source_target_pairs={{0,1},{1,0},{2,3},{3,2},{4,5},{5,4},{6,7},{7,6},{8,9},{9,8},{10,11... | collective-permute-start | bytes 3145736 | tf_op jit(solution)/shard_map/ppermute | solution.py:243
  35.1 28.3 %all-to-all-start.1 = ((bf16[32,16,128]{2,1,0:T(8,128)(2,1)}), bf16[32,16,128]{2,1,0:T(8,128)(2,1)S(1)}, u32[]{:S(2)}, u32[]{:S(2)}) async-start(bf16[32,16,128]{2,1,0:T(8,128)(2,1)} %bitcast.2), calls=%async_computation.1 | async-start | bytes 262144 | tf_op jit(solution)/shard_map/all_to_all | solution.py:234
  83.0 15.0 %copy-start.1 = (bf16[64,4096]{1,0:T(8,128)(2,1)S(1)}, bf16[64,4096]{1,0:T(8,128)(2,1)}, u32[]{:S(2)}) copy-start(bf16[64,4096]{1,0:T(8,128)(2,1)} %q_ref.5) | copy-start | bytes 1572868
  83.0 15.0 %copy-start.3 = (bf16[64,4096]{1,0:T(8,128)(2,1)S(1)}, bf16[64,4096]{1,0:T(8,128)(2,1)}, u32[]{:S(2)}) copy-start(bf16[64,4096]{1,0:T(8,128)(2,1)} %k_ref.5) | copy-start | bytes 1572868
  83.1 14.9 %copy-start.5 = (bf16[64,4096]{1,0:T(8,128)(2,1)S(1)}, bf16[64,4096]{1,0:T(8,128)(2,1)}, u32[]{:S(2)}) copy-start(bf16[64,4096]{1,0:T(8,128)(2,1)} %v_ref.5) | copy-start | bytes 1572868
  83.1 14.9 %copy-start.7 = (bf16[64,4096]{1,0:T(8,128)(2,1)S(1)}, bf16[64,4096]{1,0:T(8,128)(2,1)}, u32[]{:S(2)}) copy-start(bf16[64,4096]{1,0:T(8,128)(2,1)} %g_ref.5) | copy-start | bytes 1572868
  103.3 9.3 %collective-permute-start.1 = (bf16[3,64,2048]{2,1,0:T(8,128)(2,1)S(1)}, bf16[3,64,2048]{2,1,0:T(8,128)(2,1)S(1)}, u32[]{:S(2)}, u32[]{:S(2)}) collective-permute-start(bf16[3,64,2048]{2,1,0:T(8,128)(2,1)S(1)} %get-tuple-element.7), channel_id=1, source_target_pairs={{0,1},{1,0},{2,3},{3,2},{4,5},{5,4},{6,7},{7,6},{8,9},{9,8},{10,11... | collective-permute-start | bytes 2359304 | tf_op jit(solution)/shard_map/ppermute | solution.py:250

commit v2 on v1

v2 whole, which is shorter than its diff:
```python
import functools

import jax
import jax.numpy as jnp
from jax import lax
from jax.experimental import pallas as pl
from jax.experimental.pallas import tpu as pltpu
from jax.sharding import Mesh
from jax.sharding import PartitionSpec as P

HEADS = 32
HEAD_DIM = 128
CORES, NEAR, FAR = 2, 8, 32
HALF_HEADS = HEADS // CORES
OWNED = HALF_HEADS // NEAR
STEPS = 4
STEP_HEADS = HALF_HEADS // STEPS
F32, BF16 = jnp.float32, jnp.bfloat16
NEAR_AXES, FAR_AXES = ("zl", "x"), ("y", "zh")
BAND = 16
SMALL, LARGE = 32 * 1024 * 1024, 60 * 1024 * 1024


def params(limit=SMALL):
    return pltpu.CompilerParams(vmem_limit_bytes=limit)


def in_hbm(array):
    return pltpu.with_memory_space_constraint(array, pltpu.HBM)


def dot(a, b, contract):
    return lax.dot_general(a, b, (((contract[0],), (contract[1],)), ((), ())), preferred_element_type=F32)


def copy_all(pairs, sems):
    copies = []
    for source, target in pairs:
        for first in range(0, source.shape[0], BAND):
            band = pl.ds(first, BAND)
            copies.append(pltpu.make_async_copy(source.at[band], target.at[band], sems.at[len(copies)]))
    for copy in copies:
        copy.start()
    for copy in copies:
        copy.wait()


def pick_kernel(own, q_ref, k_ref, v_ref, g_ref, out_ref, sems):
    half = out_ref.shape[2]
    core = lax.axis_index("core")
    columns = pl.ds(pl.multiple_of((core if own else 1 - core) * half, half), half)
    copy_all([(ref.at[:, columns], out_ref.at[i]) for i, ref in enumerate((q_ref, k_ref, v_ref, g_ref))], sems)


def pick(arrays, own):
    rows, width = arrays[0].shape
    return pl.pallas_call(
        functools.partial(pick_kernel, own),
        out_shape=pltpu.VMEM((4, rows, width // CORES), BF16),
        in_specs=[pl.BlockSpec(memory_space=pltpu.HBM)] * 4,
        out_specs=pl.BlockSpec(memory_space=pltpu.VMEM),
        scratch_shapes=[pltpu.SemaphoreType.DMA((4 * rows // BAND,))],
        compiler_params=params(),
        cost_estimate=pl.CostEstimate(flops=0, bytes_accessed=2 * 4 * rows * width, transcendentals=0),
        name="own_half" if own else "other_half",
    )(*[in_hbm(array) for array in arrays])


def state_kernel(own_ref, other_ref, out_ref, held, sems):
    copies = []
    for owner in range(NEAR):
        for head in range(OWNED):
            first = (owner * OWNED + head) * HEAD_DIM
            columns = slice(first, first + HEAD_DIM)
            query, key, value, grad = [
                jnp.concatenate([own_ref[i, :, columns], other_ref[i, :, columns]], axis=0) for i in range(4)
            ]
            held[owner, 0, head] = dot(key, value, (0, 0)).astype(BF16)
            held[owner, 1, head] = dot(query, grad, (0, 0)).astype(BF16)
        copies.append(pltpu.make_async_copy(held.at[owner], out_ref.at[owner], sems.at[owner]))
        copies[-1].start()
    for copy in copies:
        copy.wait()


def chunk_states(own, other):
    shape = (NEAR, 2, OWNED, HEAD_DIM, HEAD_DIM)
    return pl.pallas_call(
        state_kernel,
        out_shape=pltpu.HBM(shape, BF16),
        in_specs=[pl.BlockSpec(memory_space=pltpu.VMEM)] * 2,
        out_specs=pl.BlockSpec(memory_space=pltpu.HBM),
        scratch_shapes=[pltpu.VMEM(shape, BF16), pltpu.SemaphoreType.DMA((NEAR,))],
        compiler_params=params(),
        name="chunk_states",
    )(own, other)


def tokens_of(refs, other_ref, head):
    columns = slice(head * HEAD_DIM, (head + 1) * HEAD_DIM)
    return [
        jnp.concatenate([ref[:, columns], other_ref[i, :, columns]], axis=0) for i, ref in enumerate(refs)
    ]


def token_specs(rows):
    columns = STEP_HEADS * HEAD_DIM
    own = pl.BlockSpec((rows, columns), lambda i, core: (0, core[0] * STEPS + i))
    other = pl.BlockSpec((4, rows, columns), lambda i, core: (0, 0, i))
    state = pl.BlockSpec((STEP_HEADS // OWNED, 2, OWNED, HEAD_DIM, HEAD_DIM), lambda i, core: (i, 0, 0, 0, 0))
    return own, other, state


def total_kernel(near_ref, out_ref):
    total = near_ref[0].astype(F32)
    for chip in range(1, NEAR):
        total += near_ref[chip].astype(F32)
    out_ref[...] = total.astype(BF16)


def group_total(near):
    return pl.pallas_call(
        total_kernel,
        out_shape=jax.ShapeDtypeStruct(near.shape[1:], BF16),
        in_specs=[pl.BlockSpec(memory_space=pltpu.VMEM)],
        out_specs=pl.BlockSpec(memory_space=pltpu.VMEM),
        compiler_params=params(),
        name="group_total",
    )(near)


def carry_kernel(far_ref, out_ref):
    place = lax.axis_index(FAR_AXES)

    @pl.when(place < FAR // 2)
    def _():
        total = jnp.zeros(far_ref.shape[1:], F32)
        for group in range(FAR):
            out_ref[group] = total.astype(BF16)
            total += far_ref[group].astype(F32)

    @pl.when(place >= FAR // 2)
    def _():
        total = jnp.zeros(far_ref.shape[1:], F32)
        for group in reversed(range(FAR)):
            out_ref[group] = total.astype(BF16)
            total += far_ref[group].astype(F32)


def group_carry(far):
    return pl.pallas_call(
        carry_kernel,
        out_shape=jax.ShapeDtypeStruct(far.shape, BF16),
        in_specs=[pl.BlockSpec(memory_space=pltpu.VMEM)],
        out_specs=pl.BlockSpec(memory_space=pltpu.VMEM),
        compiler_params=params(),
        name="group_carry",
    )(far)


def spread_kernel(near_ref, carry_ref, out_ref):
    for head in range(OWNED):
        total = carry_ref[0, head].astype(F32)
        for chip in range(NEAR):
            out_ref[chip, 0, head] = total.astype(BF16)
            total += near_ref[chip, 0, head].astype(F32)
        total = carry_ref[1, head].astype(F32)
        for chip in reversed(range(NEAR)):
            out_ref[chip, 1, head] = total.astype(BF16)
            total += near_ref[chip, 1, head].astype(F32)


def chip_carry(near, carry):
    return pl.pallas_call(
        spread_kernel,
        out_shape=jax.ShapeDtypeStruct(near.shape, BF16),
        in_specs=[pl.BlockSpec(memory_space=pltpu.VMEM)] * 2,
        out_specs=pl.BlockSpec(memory_space=pltpu.VMEM),
        compiler_params=params(),
        name="chip_carry",
    )(near, carry)


def inner_kernel(core_ref, q_ref, k_ref, v_ref, g_ref, other_ref, out_ref, kept_ref):
    rows = q_ref.shape[0]
    core = core_ref[0]

    def place(axis):
        at = lax.broadcasted_iota(jnp.int32, (2 * rows, 2 * rows), axis)
        return jnp.where(at < rows, at + core * rows, at - core * rows)

    lower = place(0) >= place(1)
    for head in range(STEP_HEADS):
        query, key, value, grad = tokens_of((q_ref, k_ref, v_ref, g_ref), other_ref, head)
        value_scores = jnp.where(lower, dot(grad, value, (1, 1)), 0.0).astype(BF16)
        key_scores = jnp.where(lower, dot(query, key, (1, 1)), 0.0).astype(BF16)
        columns = slice(head * HEAD_DIM, (head + 1) * HEAD_DIM)
        out_ref[0, :, columns] = dot(value_scores, key, (1, 0))
        out_ref[1, :, columns] = dot(value_scores, query, (0, 0))
        out_ref[2, :, columns] = dot(key_scores, grad, (0, 0))
        for i, operand in enumerate((grad, value, key)):
            kept_ref[i, :, columns] = operand


def inner_part(core, arrays, other):
    rows, width = arrays[0].shape
    own_spec, other_spec, _ = token_specs(rows)
    columns = STEP_HEADS * HEAD_DIM
    return pl.pallas_call(
        inner_kernel,
        out_shape=[pltpu.HBM((3, 2 * rows, width // CORES), dtype) for dtype in (F32, BF16)],
        grid_spec=pltpu.PrefetchScalarGridSpec(
            num_scalar_prefetch=1,
            grid=(STEPS,),
            in_specs=[own_spec] * 4 + [other_spec],
            out_specs=[pl.BlockSpec((3, 2 * rows, columns), lambda i, core: (0, 0, i))] * 2,
        ),
        compiler_params=params(LARGE),
        cost_estimate=pl.CostEstimate(
            flops=10 * HALF_HEADS * (2 * rows) ** 2 * HEAD_DIM, bytes_accessed=12 * 2**20, transcendentals=0
        ),
        name="inner_part",
    )(core, *arrays, other)


def outer_part(rows, head, inner_ref, kept_ref, carry_ref):
    columns = slice(head * HEAD_DIM, (head + 1) * HEAD_DIM)
    grad, value, key = [kept_ref[i, rows, columns] for i in range(3)]
    prior = carry_ref[head // OWNED, 0, head % OWNED]
    later = carry_ref[head // OWNED, 1, head % OWNED]
    outer = (dot(grad, prior, (1, 1)), dot(value, later, (1, 1)), dot(key, later, (1, 0)))
    return columns, [(part + inner_ref[i, rows, columns]).astype(BF16) for i, part in enumerate(outer)]


def other_kernel(inner_ref, kept_ref, carry_ref, out_ref):
    rows = out_ref.shape[1]
    for head in range(HALF_HEADS):
        columns, results = outer_part(slice(rows, 2 * rows), head, inner_ref, kept_ref, carry_ref)
        for i, result in enumerate(results):
            out_ref[i, :, columns] = result


def other_gradients(inner, kept, carry):
    _, rows, half = kept.shape
    return pl.pallas_call(
        other_kernel,
        out_shape=pltpu.VMEM((3, rows // 2, half), BF16),
        in_specs=[pl.BlockSpec(memory_space=pltpu.VMEM)] * 3,
        out_specs=pl.BlockSpec(memory_space=pltpu.VMEM),
        compiler_params=params(),
        name="other_gradients",
    )(inner, kept, carry)


def own_kernel(inner_ref, kept_ref, carry_ref, gq_ref, gk_ref, gv_ref, held, sems):
    rows, half = held.shape[1:]
    place = lax.axis_index("core") * half
    copies = []
    for head in range(HALF_HEADS):
        columns, results = outer_part(slice(0, rows), head, inner_ref, kept_ref, carry_ref)
        for i, result in enumerate(results):
            held[i, :, columns] = result
        if (head + 1) % STEP_HEADS == 0:
            width = STEP_HEADS * HEAD_DIM
            first = columns.stop - width
            for i, ref in enumerate((gq_ref, gk_ref, gv_ref)):
                target = ref.at[:, pl.ds(pl.multiple_of(place + first, width), width)]
                copies.append(
                    pltpu.make_async_copy(held.at[i, :, pl.ds(first, width)], target, sems.at[len(copies)])
                )
                copies[-1].start()
    for copy in copies:
        copy.wait()


def own_gradients(inner, kept, carry):
    _, rows, half = kept.shape
    return pl.pallas_call(
        own_kernel,
        out_shape=[pltpu.HBM((rows // 2, half * CORES), BF16)] * 3,
        in_specs=[pl.BlockSpec(memory_space=pltpu.VMEM)] * 3,
        out_specs=[pl.BlockSpec(memory_space=pltpu.HBM)] * 3,
        scratch_shapes=[pltpu.VMEM((3, rows // 2, half), BF16), pltpu.SemaphoreType.DMA((3 * STEPS,))],
        compiler_params=params(),
        cost_estimate=pl.CostEstimate(
            flops=3 * HALF_HEADS * rows * HEAD_DIM**2, bytes_accessed=4 * 2**20, transcendentals=0
        ),
        name="own_gradients",
    )(inner, kept, carry)


def place_kernel(got_ref, q_in, k_in, v_in, gq_ref, gk_ref, gv_ref, sems):
    half = got_ref.shape[2]
    columns = pl.ds(pl.multiple_of((1 - lax.axis_index("core")) * half, half), half)
    copy_all([(got_ref.at[i], ref.at[:, columns]) for i, ref in enumerate((gq_ref, gk_ref, gv_ref))], sems)


def place_half(got, grads):
    any_space = pl.BlockSpec(memory_space=pl.ANY)
    return pl.pallas_call(
        place_kernel,
        out_shape=[jax.ShapeDtypeStruct(array.shape, array.dtype) for array in grads],
        in_specs=[pl.BlockSpec(memory_space=pltpu.VMEM)] + [any_space] * 3,
        out_specs=[any_space] * 3,
        scratch_shapes=[pltpu.SemaphoreType.DMA((3 * got.shape[1] // BAND,))],
        input_output_aliases={1: 0, 2: 1, 3: 2},
        compiler_params=params(),
        name="place_half",
    )(got, *grads)


def exchange(array, axes):
    return lax.all_to_all(array, axes, split_axis=0, concat_axis=0, tiled=True)


def local(queries, keys, values, grad_out):
    arrays = (queries, keys, values, grad_out)
    swap = [(0, 1), (1, 0)]
    core = lax.axis_index("core").reshape(1)
    other = lax.ppermute(pick(arrays, False), "core", swap)
    near = exchange(chunk_states(pick(arrays, True), other), NEAR_AXES)
    near, *inner = lax.optimization_barrier((near, *inner_part(core, arrays, other)))
    total = group_total(near)
    far = exchange(total.reshape(FAR, -1, HEAD_DIM), FAR_AXES)
    carry = exchange(group_carry(far), FAR_AXES).reshape(total.shape)
    carry = exchange(chip_carry(near, carry), NEAR_AXES)
    got = lax.ppermute(other_gradients(*inner, carry), "core", swap)
    return tuple(place_half(got, own_gradients(*inner, carry)))


def solution(mesh):
    devices = mesh.devices.reshape(4, 8, 2, 4, 2)
    chips = Mesh(devices, ("y", "zh", "zl", "x", "core"))
    rows = P(("y", "zh", "zl", "x", "core"), None)
    return jax.shard_map(
        local, mesh=chips, in_specs=(rows,) * 4, out_specs=(rows,) * 3, check_vma=False
    )
```

time: 114 us -> 108 us (0.947)
  blocking collectives: 51.3 us -> 62.8 us
  starting transfers between devices: 30.4 us -> 19.4 us
  waiting for transfers between devices: 18.1 us -> 9.44 us
  Pallas kernels: 8.7 us -> 14.6 us
  local copies, waits for them, and re-layouts: 4.19 us -> 0.01 us
    all_to_all x3, blocking collectives: 51.3 us -> 62.8 us  [exchange(): return lax.all_to_all(array, axes, split_axis=0, concat_axis=0, tiled=True)]
    all_to_all x1, starting transfers between devices: 14.3 us -> 3.57 us  [exchange(): return lax.all_to_all(array, axes, split_axis=0, concat_axis=0, tiled=True)]
    pallas_call x3 -> x6, Pallas kernels: 6.81 us -> 13.3 us  [the longest x1 6.52 us: inner_part(): pl.pallas_call(inner_kernel, out_shape=[pltpu.HBM((3, 2 * rows, width //...]
    all_to_all x1, waiting for transfers between devices: 14 us -> 8.38 us  [exchange(): return lax.all_to_all(array, axes, split_axis=0, concat_axis=0, tiled=True)]
    unnamed x16 -> x6, local copies, waits for them, and re-layouts: 4.19 us -> 0.01 us
    ppermute x2, waiting for transfers between devices: 4.15 us -> 1.07 us  [the longest x1 0.87 us: local(): other = lax.ppermute(pick(arrays, False), 'core', swap)]
  transfers between devices with their start and end apart: 3 -> 3, of which waited for: 3 -> 3; matrix products, arithmetic and copies ran while one was open for 0% -> 0% of each run, Pallas kernels for 0% -> 9%
where the time goes in v2:
time: 108 us; the launch traced here: 107 us
  blocking collectives  62.8 us (58%)
  starting transfers between devices  19.4 us (18%)
  Pallas kernels  14.6 us (14%)
  waiting for transfers between devices  9.44 us (9%)
    all_to_all x3, blocking collectives, exchange(): return lax.all_to_all(array, axes, split_axis=0, concat_axis=0, tiled=True)  62.8 us
    ppermute x1, starting transfers between devices, local(): other = lax.ppermute(pick(arrays, False), 'core', swap)  8.79 us
    all_to_all x1, waiting for transfers between devices, exchange(): return lax.all_to_all(array, axes, split_axis=0, concat_axis=0, tiled=True)  8.38 us
    ppermute x1, starting transfers between devices, local(): got = lax.ppermute(other_gradients(*inner, carry), 'core', swap)  7.05 us
    pallas_call x1, Pallas kernels, inner_part(): pl.pallas_call(inner_kernel, out_shape=[pltpu.HBM((3, 2 * rows, width //...  6.52 us
    all_to_all x1, starting transfers between devices, exchange(): return lax.all_to_all(array, axes, split_axis=0, concat_axis=0, tiled=True)  3.57 us
    pallas_call x2, Pallas kernels, pick(): pl.pallas_call(functools.partial(pick_kernel, own), out_shape=pltpu.VMEM(...  2.77 us
  transfers between devices with their start and end apart: 3, of which 3 were waited for; matrix products, arithmetic and copies ran while one was open for 0% of the time, Pallas kernels for 9%

profile of v2, /device:TPU:1, one launch (start us, length us, event | category | flops | bytes accessed | tf_op | source)
XLA Modules:
  0.0 107.0 jit_solution(4633977885066315100)
XLA Ops:
  0.6 1.4 %other_half.1 = bf16[4,64,2048]{2,1,0:T(8,128)(2,1)S(1)} custom-call(bf16[64,4096]{1,0:T(8,128)(2,1)} %q_ref.5, bf16[64,4096]{1,0:T(8,128)(2,1)} %k_ref.5, bf16[64,4096]{1,0:T(8,128)(2,1)} %v_ref.5, bf16[64,4096]{1,0:T(8,128)(2,1)} %g_ref.5), custom_call_target="tpu_custom_call" | custom-call | bytes 2097152 | tf_op jit(solution)/shard_map/other_half/pallas_call | solution.py:57
  2.0 8.8 %collective-permute-start = (bf16[4,64,2048]{2,1,0:T(8,128)(2,1)S(1)}, bf16[4,64,2048]{2,1,0:T(8,128)(2,1)S(1)}, u32[]{:S(2)}, u32[]{:S(2)}) collective-permute-start(bf16[4,64,2048]{2,1,0:T(8,128)(2,1)S(1)} %other_half.1), channel_id=1, source_target_pairs={{0,1},{1,0},{2,3},{3,2},{4,5},{5,4},{6,7},{7,6},{8,9},{9,8},{10,11... | collective-permute-start | bytes 3145736 | tf_op jit(solution)/shard_map/ppermute | solution.py:320
  10.8 1.4 %own_half.1.own_ref = bf16[4,64,2048]{2,1,0:T(8,128)(2,1)S(1)} custom-call(bf16[64,4096]{1,0:T(8,128)(2,1)} %q_ref.5, bf16[64,4096]{1,0:T(8,128)(2,1)} %k_ref.5, bf16[64,4096]{1,0:T(8,128)(2,1)} %v_ref.5, bf16[64,4096]{1,0:T(8,128)(2,1)} %g_ref.5), custom_call_target="tpu_custom_call" | custom-call | bytes 2097152 | tf_op jit(solution)/shard_map/own_half/pallas_call | solution.py:57
  12.2 0.9 collective-permute-done.other_ref
  13.1 0.0 copy-start.2
  13.1 1.5 %chunk_states.1 = bf16[8,2,2,128,128]{4,3,2,1,0:T(8,128)(2,1)} custom-call(bf16[4,64,2048]{2,1,0:T(8,128)(2,1)S(1)} %own_half.1.own_ref, bf16[4,64,2048]{2,1,0:T(8,128)(2,1)S(1)} %collective-permute-done.other_ref), custom_call_target="tpu_custom_call" | custom-call | tf_op jit(solution)/shard_map/chunk_states/pallas_call | solution.py:88
  14.5 3.6 %all-to-all-start = ((bf16[8,2,2,128,128]{4,3,2,1,0:T(8,128)(2,1)}), bf16[8,2,2,128,128]{4,3,2,1,0:T(8,128)(2,1)S(1)}, u32[]{:S(2)}, u32[]{:S(2)}) async-start(bf16[8,2,2,128,128]{4,3,2,1,0:T(8,128)(2,1)} %chunk_states.1), calls=%async_computation | async-start | bytes 2097152 | tf_op jit(solution)/shard_map/all_to_all | solution.py:313
  18.1 0.0 copy-done.2
  18.1 6.5 %inner_part.1 = (f32[3,128,2048]{2,1,0:T(8,128)}, bf16[3,128,2048]{2,1,0:T(8,128)(2,1)}) custom-call(s32[1]{0:T(128)} %bitcast.core_ref, bf16[64,4096]{1,0:T(8,128)(2,1)} %q_ref.5, bf16[64,4096]{1,0:T(8,128)(2,1)} %k_ref.5, bf16[64,4096]{1,0:T(8,128)(2,1)} %v_ref.5, bf16[64,4096]{1,0:T(8,128)(2,1)} %g_ref.5, bf16[4,64,2048]{2,1,0:T(8,128)(2,1)} %copy-done.2), custom_call_target="tpu_custom_call" | custom-call | flops 335544320 | bytes 12582912 | tf_op jit(solution)/shard_map/inner_part/pallas_call | solution.py:209
  24.7 8.4 %all-to-all-done.near_ref = bf16[8,2,2,128,128]{4,3,2,1,0:T(8,128)(2,1)S(1)} async-done(((bf16[8,2,2,128,128]{4,3,2,1,0:T(8,128)(2,1)}), bf16[8,2,2,128,128]{4,3,2,1,0:T(8,128)(2,1)S(1)}, u32[]{:S(2)}, u32[]{:S(2)}) %all-to-all-start) | async-done | bytes 1048608 | tf_op jit(solution)/shard_map/all_to_all | solution.py:313
  33.0 0.0 copy-start
  33.0 0.0 copy-start.1
  33.0 0.1 group_total.1
  33.2 27.6 %all_to_all.20.far_ref = bf16[32,16,128]{2,1,0:T(8,128)(2,1)S(1)} all-to-all(bf16[32,16,128]{2,1,0:T(8,128)(2,1)S(1)} %bitcast.4), channel_id=1, replica_groups=mesh['y'=4,'zh'=8,'zl'=2,'x'=4,'core'=2] {'y','zh'}, dimensions={0} | all-to-all | bytes 262144 | tf_op jit(solution)/shard_map/all_to_all | solution.py:313
  60.9 20.6 %all_to_all.21 = bf16[32,16,128]{2,1,0:T(8,128)(2,1)S(1)} all-to-all(bf16[32,16,128]{2,1,0:T(8,128)(2,1)S(1)} %group_carry.1), channel_id=1, replica_groups=mesh['y'=4,'zh'=8,'zl'=2,'x'=4,'core'=2] {'y','zh'}, dimensions={0} | all-to-all | bytes 262144 | tf_op jit(solution)/shard_map/all_to_all | solution.py:313
  81.4 0.2 chip_carry.1
  81.6 14.6 %all_to_all.22.carry_ref = bf16[8,2,2,128,128]{4,3,2,1,0:T(8,128)(2,1)S(1)} all-to-all(bf16[8,2,2,128,128]{4,3,2,1,0:T(8,128)(2,1)S(1)} %chip_carry.1), channel_id=1, replica_groups=mesh['y'=4,'zh'=8,'zl'=2,'x'=4,'core'=2] {'zl','x'}, dimensions={0} | all-to-all | bytes 2097152 | tf_op jit(solution)/shard_map/all_to_all | solution.py:313
  96.2 0.0 copy-done
  96.2 0.0 copy-done.1
  96.2 0.9 other_gradients.1
  97.1 7.1 %collective-permute-start.1 = (bf16[3,64,2048]{2,1,0:T(8,128)(2,1)S(1)}, bf16[3,64,2048]{2,1,0:T(8,128)(2,1)S(1)}, u32[]{:S(2)}, u32[]{:S(2)}) collective-permute-start(bf16[3,64,2048]{2,1,0:T(8,128)(2,1)S(1)} %other_gradients.1), channel_id=1, source_target_pairs={{0,1},{1,0},{2,3},{3,2},{4,5},{5,4},{6,7},{7,6},{8,9},{9,8},{10,11... | collective-permute-start | bytes 2359304 | tf_op jit(solution)/shard_map/ppermute | solution.py:327
  104.2 1.7 %own_gradients.1 = (bf16[64,4096]{1,0:T(8,128)(2,1)}, bf16[64,4096]{1,0:T(8,128)(2,1)}, bf16[64,4096]{1,0:T(8,128)(2,1)}) custom-call(f32[3,128,2048]{2,1,0:T(8,128)S(1)} %copy-done, bf16[3,128,2048]{2,1,0:T(8,128)(2,1)S(1)} %copy-done.1, bf16[8,2,2,128,128]{4,3,2,1,0:T(8,128)(2,1)S(1)} %all_to_all.22.carry_ref), custom_call_target="tpu_custom_call" | custom-call | flops 100663296 | bytes 4194304 | tf_op jit(solution)/shard_map/own_gradients/pallas_call | solution.py:278
  105.9 0.2 collective-permute-done.1.got_ref
  106.1 1.0 place_half.1
  (1 shorter events, 0.0 us)
Async XLA Ops:
  2.0 11.1 %collective-permute-start = (bf16[4,64,2048]{2,1,0:T(8,128)(2,1)S(1)}, bf16[4,64,2048]{2,1,0:T(8,128)(2,1)S(1)}, u32[]{:S(2)}, u32[]{:S(2)}) collective-permute-start(bf16[4,64,2048]{2,1,0:T(8,128)(2,1)S(1)} %other_half.1), channel_id=1, source_target_pairs={{0,1},{1,0},{2,3},{3,2},{4,5},{5,4},{6,7},{7,6},{8,9},{9,8},{10,11... | collective-permute-start | bytes 3145736 | tf_op jit(solution)/shard_map/ppermute | solution.py:320
  13.1 5.0 %copy-start.2 = (bf16[4,64,2048]{2,1,0:T(8,128)(2,1)}, bf16[4,64,2048]{2,1,0:T(8,128)(2,1)S(1)}, u32[]{:S(2)}) copy-start(bf16[4,64,2048]{2,1,0:T(8,128)(2,1)S(1)} %collective-permute-done.other_ref) | copy-start | bytes 3145732
  14.5 18.5 %all-to-all-start = ((bf16[8,2,2,128,128]{4,3,2,1,0:T(8,128)(2,1)}), bf16[8,2,2,128,128]{4,3,2,1,0:T(8,128)(2,1)S(1)}, u32[]{:S(2)}, u32[]{:S(2)}) async-start(bf16[8,2,2,128,128]{4,3,2,1,0:T(8,128)(2,1)} %chunk_states.1), calls=%async_computation | async-start | bytes 2097152 | tf_op jit(solution)/shard_map/all_to_all | solution.py:313
  33.0 63.2 %copy-start = (f32[3,128,2048]{2,1,0:T(8,128)S(1)}, f32[3,128,2048]{2,1,0:T(8,128)}, u32[]{:S(2)}) copy-start(f32[3,128,2048]{2,1,0:T(8,128)} %get-tuple-element.13.inner_ref) | copy-start | bytes 9437188
  33.0 63.2 %copy-start.1 = (bf16[3,128,2048]{2,1,0:T(8,128)(2,1)S(1)}, bf16[3,128,2048]{2,1,0:T(8,128)(2,1)}, u32[]{:S(2)}) copy-start(bf16[3,128,2048]{2,1,0:T(8,128)(2,1)} %get-tuple-element.14.kept_ref) | copy-start | bytes 4718596
  97.1 9.0 %collective-permute-start.1 = (bf16[3,64,2048]{2,1,0:T(8,128)(2,1)S(1)}, bf16[3,64,2048]{2,1,0:T(8,128)(2,1)S(1)}, u32[]{:S(2)}, u32[]{:S(2)}) collective-permute-start(bf16[3,64,2048]{2,1,0:T(8,128)(2,1)S(1)} %other_gradients.1), channel_id=1, source_target_pairs={{0,1},{1,0},{2,3},{3,2},{4,5},{5,4},{6,7},{7,6},{8,9},{9,8},{10,11... | collective-permute-start | bytes 2359304 | tf_op jit(solution)/shard_map/ppermute | solution.py:327

commit v3 on v2

--- a/solution.py
+++ b/solution.py
@@ -17,7 +17,7 @@
 STEP_HEADS = HALF_HEADS // STEPS
 F32, BF16 = jnp.float32, jnp.bfloat16
 NEAR_AXES, FAR_AXES = ("zl", "x"), ("y", "zh")
-BAND = 16
+BAND = 64
 SMALL, LARGE = 32 * 1024 * 1024, 60 * 1024 * 1024
 
 

time: 108 us -> 107 us (level)
  no operation moved by 1% of the time
where the time goes in v3:
time: 107 us
  blocking collectives  62.8 us (59%)
  starting transfers between devices  19.4 us (18%)
  Pallas kernels  14.3 us (13%)
  waiting for transfers between devices  9.6 us (9%)
    all_to_all x3, blocking collectives, exchange(): return lax.all_to_all(array, axes, split_axis=0, concat_axis=0, tiled=True)  62.8 us
    ppermute x1, starting transfers between devices, local(): other = lax.ppermute(pick(arrays, False), 'core', swap)  8.79 us
    all_to_all x1, waiting for transfers between devices, exchange(): return lax.all_to_all(array, axes, split_axis=0, concat_axis=0, tiled=True)  8.38 us
    ppermute x1, starting transfers between devices, local(): got = lax.ppermute(other_gradients(*inner, carry), 'core', swap)  7.05 us
    pallas_call x1, Pallas kernels, inner_part(): pl.pallas_call(inner_kernel, out_shape=[pltpu.HBM((3, 2 * rows, width //...  6.52 us
    all_to_all x1, starting transfers between devices, exchange(): return lax.all_to_all(array, axes, split_axis=0, concat_axis=0, tiled=True)  3.57 us
    pallas_call x2, Pallas kernels, pick(): pl.pallas_call(functools.partial(pick_kernel, own), out_shape=pltpu.VMEM(...  2.46 us
  transfers between devices with their start and end apart: 3, of which 3 were waited for; matrix products, arithmetic and copies ran while one was open for 0% of the time, Pallas kernels for 9%

profile of v3, /device:TPU:1, one launch (start us, length us, event | category | flops | bytes accessed | tf_op | source)
XLA Modules:
  0.0 106.8 jit_solution(1530335088943448626)
XLA Ops:
  0.6 1.2 %other_half.1 = bf16[4,64,2048]{2,1,0:T(8,128)(2,1)S(1)} custom-call(bf16[64,4096]{1,0:T(8,128)(2,1)} %q_ref.5, bf16[64,4096]{1,0:T(8,128)(2,1)} %k_ref.5, bf16[64,4096]{1,0:T(8,128)(2,1)} %v_ref.5, bf16[64,4096]{1,0:T(8,128)(2,1)} %g_ref.5), custom_call_target="tpu_custom_call" | custom-call | bytes 2097152 | tf_op jit(solution)/shard_map/other_half/pallas_call | solution.py:57
  1.9 8.8 %collective-permute-start = (bf16[4,64,2048]{2,1,0:T(8,128)(2,1)S(1)}, bf16[4,64,2048]{2,1,0:T(8,128)(2,1)S(1)}, u32[]{:S(2)}, u32[]{:S(2)}) collective-permute-start(bf16[4,64,2048]{2,1,0:T(8,128)(2,1)S(1)} %other_half.1), channel_id=1, source_target_pairs={{0,1},{1,0},{2,3},{3,2},{4,5},{5,4},{6,7},{7,6},{8,9},{9,8},{10,11... | collective-permute-start | bytes 3145736 | tf_op jit(solution)/shard_map/ppermute | solution.py:320
  10.7 1.2 %own_half.1.own_ref = bf16[4,64,2048]{2,1,0:T(8,128)(2,1)S(1)} custom-call(bf16[64,4096]{1,0:T(8,128)(2,1)} %q_ref.5, bf16[64,4096]{1,0:T(8,128)(2,1)} %k_ref.5, bf16[64,4096]{1,0:T(8,128)(2,1)} %v_ref.5, bf16[64,4096]{1,0:T(8,128)(2,1)} %g_ref.5), custom_call_target="tpu_custom_call" | custom-call | bytes 2097152 | tf_op jit(solution)/shard_map/own_half/pallas_call | solution.py:57
  11.9 1.0 collective-permute-done.other_ref
  12.9 0.0 copy-start.2
  12.9 1.5 %chunk_states.1 = bf16[8,2,2,128,128]{4,3,2,1,0:T(8,128)(2,1)} custom-call(bf16[4,64,2048]{2,1,0:T(8,128)(2,1)S(1)} %own_half.1.own_ref, bf16[4,64,2048]{2,1,0:T(8,128)(2,1)S(1)} %collective-permute-done.other_ref), custom_call_target="tpu_custom_call" | custom-call | tf_op jit(solution)/shard_map/chunk_states/pallas_call | solution.py:88
  14.4 3.6 %all-to-all-start = ((bf16[8,2,2,128,128]{4,3,2,1,0:T(8,128)(2,1)}), bf16[8,2,2,128,128]{4,3,2,1,0:T(8,128)(2,1)S(1)}, u32[]{:S(2)}, u32[]{:S(2)}) async-start(bf16[8,2,2,128,128]{4,3,2,1,0:T(8,128)(2,1)} %chunk_states.1), calls=%async_computation | async-start | bytes 2097152 | tf_op jit(solution)/shard_map/all_to_all | solution.py:313
  18.0 0.0 copy-done.2
  18.0 6.5 %inner_part.1 = (f32[3,128,2048]{2,1,0:T(8,128)}, bf16[3,128,2048]{2,1,0:T(8,128)(2,1)}) custom-call(s32[1]{0:T(128)} %bitcast.core_ref, bf16[64,4096]{1,0:T(8,128)(2,1)} %q_ref.5, bf16[64,4096]{1,0:T(8,128)(2,1)} %k_ref.5, bf16[64,4096]{1,0:T(8,128)(2,1)} %v_ref.5, bf16[64,4096]{1,0:T(8,128)(2,1)} %g_ref.5, bf16[4,64,2048]{2,1,0:T(8,128)(2,1)} %copy-done.2), custom_call_target="tpu_custom_call" | custom-call | flops 335544320 | bytes 12582912 | tf_op jit(solution)/shard_map/inner_part/pallas_call | solution.py:209
  24.5 8.4 %all-to-all-done.near_ref = bf16[8,2,2,128,128]{4,3,2,1,0:T(8,128)(2,1)S(1)} async-done(((bf16[8,2,2,128,128]{4,3,2,1,0:T(8,128)(2,1)}), bf16[8,2,2,128,128]{4,3,2,1,0:T(8,128)(2,1)S(1)}, u32[]{:S(2)}, u32[]{:S(2)}) %all-to-all-start) | async-done | bytes 1048608 | tf_op jit(solution)/shard_map/all_to_all | solution.py:313
  32.9 0.0 copy-start
  32.9 0.0 copy-start.1
  32.9 0.1 group_total.1
  33.0 27.6 %all_to_all.20.far_ref = bf16[32,16,128]{2,1,0:T(8,128)(2,1)S(1)} all-to-all(bf16[32,16,128]{2,1,0:T(8,128)(2,1)S(1)} %bitcast.4), channel_id=1, replica_groups=mesh['y'=4,'zh'=8,'zl'=2,'x'=4,'core'=2] {'y','zh'}, dimensions={0} | all-to-all | bytes 262144 | tf_op jit(solution)/shard_map/all_to_all | solution.py:313
  60.7 20.6 %all_to_all.21 = bf16[32,16,128]{2,1,0:T(8,128)(2,1)S(1)} all-to-all(bf16[32,16,128]{2,1,0:T(8,128)(2,1)S(1)} %group_carry.1), channel_id=1, replica_groups=mesh['y'=4,'zh'=8,'zl'=2,'x'=4,'core'=2] {'y','zh'}, dimensions={0} | all-to-all | bytes 262144 | tf_op jit(solution)/shard_map/all_to_all | solution.py:313
  81.3 0.2 chip_carry.1
  81.4 14.6 %all_to_all.22.carry_ref = bf16[8,2,2,128,128]{4,3,2,1,0:T(8,128)(2,1)S(1)} all-to-all(bf16[8,2,2,128,128]{4,3,2,1,0:T(8,128)(2,1)S(1)} %chip_carry.1), channel_id=1, replica_groups=mesh['y'=4,'zh'=8,'zl'=2,'x'=4,'core'=2] {'zl','x'}, dimensions={0} | all-to-all | bytes 2097152 | tf_op jit(solution)/shard_map/all_to_all | solution.py:313
  96.1 0.0 copy-done
  96.1 0.0 copy-done.1
  96.1 0.9 other_gradients.1
  97.0 7.1 %collective-permute-start.1 = (bf16[3,64,2048]{2,1,0:T(8,128)(2,1)S(1)}, bf16[3,64,2048]{2,1,0:T(8,128)(2,1)S(1)}, u32[]{:S(2)}, u32[]{:S(2)}) collective-permute-start(bf16[3,64,2048]{2,1,0:T(8,128)(2,1)S(1)} %other_gradients.1), channel_id=1, source_target_pairs={{0,1},{1,0},{2,3},{3,2},{4,5},{5,4},{6,7},{7,6},{8,9},{9,8},{10,11... | collective-permute-start | bytes 2359304 | tf_op jit(solution)/shard_map/ppermute | solution.py:327
  104.0 1.7 %own_gradients.1 = (bf16[64,4096]{1,0:T(8,128)(2,1)}, bf16[64,4096]{1,0:T(8,128)(2,1)}, bf16[64,4096]{1,0:T(8,128)(2,1)}) custom-call(f32[3,128,2048]{2,1,0:T(8,128)S(1)} %copy-done, bf16[3,128,2048]{2,1,0:T(8,128)(2,1)S(1)} %copy-done.1, bf16[8,2,2,128,128]{4,3,2,1,0:T(8,128)(2,1)S(1)} %all_to_all.22.carry_ref), custom_call_target="tpu_custom_call" | custom-call | flops 100663296 | bytes 4194304 | tf_op jit(solution)/shard_map/own_gradients/pallas_call | solution.py:278
  105.7 0.2 collective-permute-done.1.got_ref
  105.9 0.9 place_half.1
  (1 shorter events, 0.0 us)
Async XLA Ops:
  1.9 11.1 %collective-permute-start = (bf16[4,64,2048]{2,1,0:T(8,128)(2,1)S(1)}, bf16[4,64,2048]{2,1,0:T(8,128)(2,1)S(1)}, u32[]{:S(2)}, u32[]{:S(2)}) collective-permute-start(bf16[4,64,2048]{2,1,0:T(8,128)(2,1)S(1)} %other_half.1), channel_id=1, source_target_pairs={{0,1},{1,0},{2,3},{3,2},{4,5},{5,4},{6,7},{7,6},{8,9},{9,8},{10,11... | collective-permute-start | bytes 3145736 | tf_op jit(solution)/shard_map/ppermute | solution.py:320
  12.9 5.0 %copy-start.2 = (bf16[4,64,2048]{2,1,0:T(8,128)(2,1)}, bf16[4,64,2048]{2,1,0:T(8,128)(2,1)S(1)}, u32[]{:S(2)}) copy-start(bf16[4,64,2048]{2,1,0:T(8,128)(2,1)S(1)} %collective-permute-done.other_ref) | copy-start | bytes 3145732
  14.4 18.5 %all-to-all-start = ((bf16[8,2,2,128,128]{4,3,2,1,0:T(8,128)(2,1)}), bf16[8,2,2,128,128]{4,3,2,1,0:T(8,128)(2,1)S(1)}, u32[]{:S(2)}, u32[]{:S(2)}) async-start(bf16[8,2,2,128,128]{4,3,2,1,0:T(8,128)(2,1)} %chunk_states.1), calls=%async_computation | async-start | bytes 2097152 | tf_op jit(solution)/shard_map/all_to_all | solution.py:313
  32.9 63.2 %copy-start = (f32[3,128,2048]{2,1,0:T(8,128)S(1)}, f32[3,128,2048]{2,1,0:T(8,128)}, u32[]{:S(2)}) copy-start(f32[3,128,2048]{2,1,0:T(8,128)} %get-tuple-element.13.inner_ref) | copy-start | bytes 9437188
  32.9 63.2 %copy-start.1 = (bf16[3,128,2048]{2,1,0:T(8,128)(2,1)S(1)}, bf16[3,128,2048]{2,1,0:T(8,128)(2,1)}, u32[]{:S(2)}) copy-start(bf16[3,128,2048]{2,1,0:T(8,128)(2,1)} %get-tuple-element.14.kept_ref) | copy-start | bytes 4718596
  97.0 8.9 %collective-permute-start.1 = (bf16[3,64,2048]{2,1,0:T(8,128)(2,1)S(1)}, bf16[3,64,2048]{2,1,0:T(8,128)(2,1)S(1)}, u32[]{:S(2)}, u32[]{:S(2)}) collective-permute-start(bf16[3,64,2048]{2,1,0:T(8,128)(2,1)S(1)} %other_gradients.1), channel_id=1, source_target_pairs={{0,1},{1,0},{2,3},{3,2},{4,5},{5,4},{6,7},{7,6},{8,9},{9,8},{10,11... | collective-permute-start | bytes 2359304 | tf_op jit(solution)/shard_map/ppermute | solution.py:327

commit v4 on v3

--- a/solution.py
+++ b/solution.py
@@ -10,13 +10,14 @@
 
 HEADS = 32
 HEAD_DIM = 128
-CORES, NEAR, FAR = 2, 8, 32
+CORES, SPANS_Y, NEAR_Y, CHIPS, FAR_Z, BLOCK = 2, 4, 4, 8, 8, 16
+NEAR, FAR = NEAR_Y * CHIPS, SPANS_Y // NEAR_Y * FAR_Z
 HALF_HEADS = HEADS // CORES
-OWNED = HALF_HEADS // NEAR
+OWNED_ROWS = HALF_HEADS * HEAD_DIM // NEAR
 STEPS = 4
 STEP_HEADS = HALF_HEADS // STEPS
 F32, BF16 = jnp.float32, jnp.bfloat16
-NEAR_AXES, FAR_AXES = ("zl", "x"), ("y", "zh")
+NEAR_AXES, FAR_AXES = ("yn", "zl", "x"), ("yf", "zh")
 BAND = 64
 SMALL, LARGE = 32 * 1024 * 1024, 60 * 1024 * 1024
 
@@ -68,29 +69,46 @@
 
 def state_kernel(own_ref, other_ref, out_ref, held, sems):
     copies = []
-    for owner in range(NEAR):
-        for head in range(OWNED):
-            first = (owner * OWNED + head) * HEAD_DIM
-            columns = slice(first, first + HEAD_DIM)
-            query, key, value, grad = [
-                jnp.concatenate([own_ref[i, :, columns], other_ref[i, :, columns]], axis=0) for i in range(4)
-            ]
-            held[owner, 0, head] = dot(key, value, (0, 0)).astype(BF16)
-            held[owner, 1, head] = dot(query, grad, (0, 0)).astype(BF16)
-        copies.append(pltpu.make_async_copy(held.at[owner], out_ref.at[owner], sems.at[owner]))
-        copies[-1].start()
+    for head in range(HALF_HEADS):
+        columns = slice(head * HEAD_DIM, (head + 1) * HEAD_DIM)
+        query, key, value, grad = [
+            jnp.concatenate([own_ref[i, :, columns], other_ref[i, :, columns]], axis=0) for i in range(4)
+        ]
+        for i, state in enumerate((dot(key, value, (0, 0)), dot(query, grad, (0, 0)))):
+            write_state(held, head, i, state.astype(BF16))
+        if (head + 1) % 2 == 0:
+            share = pl.ds((head - 1) * NEAR // HALF_HEADS, 2 * NEAR // HALF_HEADS)
+            copies.append(pltpu.make_async_copy(held.at[share], out_ref.at[share], sems.at[len(copies)]))
+            copies[-1].start()
     for copy in copies:
         copy.wait()
 
 
+def write_state(ref, head, i, state):
+    first = head * HEAD_DIM
+    for row in range(0, HEAD_DIM, min(HEAD_DIM, OWNED_ROWS)):
+        owner, at = divmod(first + row, OWNED_ROWS)
+        count = min(HEAD_DIM, OWNED_ROWS)
+        ref[owner, i, at : at + count] = state[row : row + count]
+
+
+def read_state(ref, head, i):
+    first, count = head * HEAD_DIM, min(HEAD_DIM, OWNED_ROWS)
+    parts = []
+    for row in range(0, HEAD_DIM, count):
+        owner, at = divmod(first + row, OWNED_ROWS)
+        parts.append(ref[owner, i, at : at + count])
+    return parts[0] if len(parts) == 1 else jnp.concatenate(parts, axis=0)
+
+
 def chunk_states(own, other):
-    shape = (NEAR, 2, OWNED, HEAD_DIM, HEAD_DIM)
+    shape = (NEAR, 2, OWNED_ROWS, HEAD_DIM)
     return pl.pallas_call(
         state_kernel,
         out_shape=pltpu.HBM(shape, BF16),
         in_specs=[pl.BlockSpec(memory_space=pltpu.VMEM)] * 2,
         out_specs=pl.BlockSpec(memory_space=pltpu.HBM),
-        scratch_shapes=[pltpu.VMEM(shape, BF16), pltpu.SemaphoreType.DMA((NEAR,))],
+        scratch_shapes=[pltpu.VMEM(shape, BF16), pltpu.SemaphoreType.DMA((HALF_HEADS // 2,))],
         compiler_params=params(),
         name="chunk_states",
     )(own, other)
@@ -107,21 +125,25 @@
     columns = STEP_HEADS * HEAD_DIM
     own = pl.BlockSpec((rows, columns), lambda i, core: (0, core[0] * STEPS + i))
     other = pl.BlockSpec((4, rows, columns), lambda i, core: (0, 0, i))
-    state = pl.BlockSpec((STEP_HEADS // OWNED, 2, OWNED, HEAD_DIM, HEAD_DIM), lambda i, core: (i, 0, 0, 0, 0))
-    return own, other, state
+    return own, other
 
 
 def total_kernel(near_ref, out_ref):
-    total = near_ref[0].astype(F32)
-    for chip in range(1, NEAR):
-        total += near_ref[chip].astype(F32)
-    out_ref[...] = total.astype(BF16)
+    half = FAR // 2
+    for span in range(NEAR_Y):
+        total = near_ref[span * CHIPS].astype(F32)
+        for chip in range(1, CHIPS):
+            total += near_ref[span * CHIPS + chip].astype(F32)
+        total = total.astype(BF16)
+        for slot in range(FAR):
+            block = slot % half * BLOCK
+            out_ref[slot, span] = total[slot // half, block : block + BLOCK]
 
 
 def group_total(near):
     return pl.pallas_call(
         total_kernel,
-        out_shape=jax.ShapeDtypeStruct(near.shape[1:], BF16),
+        out_shape=pltpu.VMEM((FAR, NEAR_Y, BLOCK, HEAD_DIM), BF16),
         in_specs=[pl.BlockSpec(memory_space=pltpu.VMEM)],
         out_specs=pl.BlockSpec(memory_space=pltpu.VMEM),
         compiler_params=params(),
@@ -129,28 +151,36 @@
     )(near)
 
 
+def groups_in_order():
+    order = []
+    for y in range(SPANS_Y):
+        far_at, near_at = divmod(y, NEAR_Y)
+        order += [(far_at * FAR_Z + z, near_at) for z in range(FAR_Z)]
+    return order
+
+
 def carry_kernel(far_ref, out_ref):
     place = lax.axis_index(FAR_AXES)
 
+    def run(order):
+        total = jnp.zeros((BLOCK, HEAD_DIM), F32)
+        for group in order:
+            out_ref[group] = total.astype(BF16)
+            total += far_ref[group].astype(F32)
+
     @pl.when(place < FAR // 2)
     def _():
-        total = jnp.zeros(far_ref.shape[1:], F32)
-        for group in range(FAR):
-            out_ref[group] = total.astype(BF16)
-            total += far_ref[group].astype(F32)
+        run(groups_in_order())
 
     @pl.when(place >= FAR // 2)
     def _():
-        total = jnp.zeros(far_ref.shape[1:], F32)
-        for group in reversed(range(FAR)):
-            out_ref[group] = total.astype(BF16)
-            total += far_ref[group].astype(F32)
+        run(groups_in_order()[::-1])
 
 
 def group_carry(far):
     return pl.pallas_call(
         carry_kernel,
-        out_shape=jax.ShapeDtypeStruct(far.shape, BF16),
+        out_shape=pltpu.VMEM(far.shape, BF16),
         in_specs=[pl.BlockSpec(memory_space=pltpu.VMEM)],
         out_specs=pl.BlockSpec(memory_space=pltpu.VMEM),
         compiler_params=params(),
@@ -159,21 +189,19 @@
 
 
 def spread_kernel(near_ref, carry_ref, out_ref):
-    for head in range(OWNED):
-        total = carry_ref[0, head].astype(F32)
-        for chip in range(NEAR):
-            out_ref[chip, 0, head] = total.astype(BF16)
-            total += near_ref[chip, 0, head].astype(F32)
-        total = carry_ref[1, head].astype(F32)
-        for chip in reversed(range(NEAR)):
-            out_ref[chip, 1, head] = total.astype(BF16)
-            total += near_ref[chip, 1, head].astype(F32)
+    half = FAR // 2
+    for span in range(NEAR_Y):
+        for i, order in enumerate((range(CHIPS), range(CHIPS)[::-1])):
+            total = jnp.concatenate([carry_ref[i * half + j, span] for j in range(half)], axis=0).astype(F32)
+            for chip in order:
+                out_ref[span * CHIPS + chip, i] = total.astype(BF16)
+                total += near_ref[span * CHIPS + chip, i].astype(F32)
 
 
 def chip_carry(near, carry):
     return pl.pallas_call(
         spread_kernel,
-        out_shape=jax.ShapeDtypeStruct(near.shape, BF16),
+        out_shape=pltpu.VMEM(near.shape, BF16),
         in_specs=[pl.BlockSpec(memory_space=pltpu.VMEM)] * 2,
         out_specs=pl.BlockSpec(memory_space=pltpu.VMEM),
         compiler_params=params(),
@@ -204,7 +232,7 @@
 
 def inner_part(core, arrays, other):
     rows, width = arrays[0].shape
-    own_spec, other_spec, _ = token_specs(rows)
+    own_spec, other_spec = token_specs(rows)
     columns = STEP_HEADS * HEAD_DIM
     return pl.pallas_call(
         inner_kernel,
@@ -226,8 +254,7 @@
 def outer_part(rows, head, inner_ref, kept_ref, carry_ref):
     columns = slice(head * HEAD_DIM, (head + 1) * HEAD_DIM)
     grad, value, key = [kept_ref[i, rows, columns] for i in range(3)]
-    prior = carry_ref[head // OWNED, 0, head % OWNED]
-    later = carry_ref[head // OWNED, 1, head % OWNED]
+    prior, later = read_state(carry_ref, head, 0), read_state(carry_ref, head, 1)
     outer = (dot(grad, prior, (1, 1)), dot(value, later, (1, 1)), dot(key, later, (1, 0)))
     return columns, [(part + inner_ref[i, rows, columns]).astype(BF16) for i, part in enumerate(outer)]
 
@@ -320,18 +347,18 @@
     other = lax.ppermute(pick(arrays, False), "core", swap)
     near = exchange(chunk_states(pick(arrays, True), other), NEAR_AXES)
     near, *inner = lax.optimization_barrier((near, *inner_part(core, arrays, other)))
-    total = group_total(near)
-    far = exchange(total.reshape(FAR, -1, HEAD_DIM), FAR_AXES)
-    carry = exchange(group_carry(far), FAR_AXES).reshape(total.shape)
+    far = exchange(group_total(near), FAR_AXES)
+    carry = exchange(group_carry(far), FAR_AXES)
     carry = exchange(chip_carry(near, carry), NEAR_AXES)
     got = lax.ppermute(other_gradients(*inner, carry), "core", swap)
     return tuple(place_half(got, own_gradients(*inner, carry)))
 
 
 def solution(mesh):
-    devices = mesh.devices.reshape(4, 8, 2, 4, 2)
-    chips = Mesh(devices, ("y", "zh", "zl", "x", "core"))
-    rows = P(("y", "zh", "zl", "x", "core"), None)
+    sizes = {"yf": SPANS_Y // NEAR_Y, "yn": NEAR_Y, "zh": FAR_Z, "zl": 2, "x": 4, "core": CORES}
+    names = tuple(sizes)
+    chips = Mesh(mesh.devices.reshape(tuple(sizes.values())), names)
+    rows = P(names, None)
     return jax.shard_map(
         local, mesh=chips, in_specs=(rows,) * 4, out_specs=(rows,) * 3, check_vma=False
     )

time: 107 us -> 106 us (level)
  blocking collectives: 62.8 us -> 61.1 us
  waiting for transfers between devices: 9.6 us -> 10.8 us
    all_to_all x3, blocking collectives: 62.8 us -> 61.1 us  [exchange(): return lax.all_to_all(array, axes, split_axis=0, concat_axis=0, tiled=True)]
    all_to_all x1, waiting for transfers between devices: 8.38 us -> 9.55 us  [exchange(): return lax.all_to_all(array, axes, split_axis=0, concat_axis=0, tiled=True)]
where the time goes in v4:
time: 106 us
  blocking collectives  61.1 us (58%)
  starting transfers between devices  19 us (18%)
  Pallas kernels  14.3 us (13%)
  waiting for transfers between devices  10.8 us (10%)
    all_to_all x3, blocking collectives, exchange(): return lax.all_to_all(array, axes, split_axis=0, concat_axis=0, tiled=True)  61.1 us
    all_to_all x1, waiting for transfers between devices, exchange(): return lax.all_to_all(array, axes, split_axis=0, concat_axis=0, tiled=True)  9.55 us
    ppermute x1, starting transfers between devices, local(): other = lax.ppermute(pick(arrays, False), 'core', swap)  8.79 us
    pallas_call x1, Pallas kernels, inner_part(): pl.pallas_call(inner_kernel, out_shape=[pltpu.HBM((3, 2 * rows, width //...  6.52 us
    ppermute x1, starting transfers between devices, local(): got = lax.ppermute(other_gradients(*inner, carry), 'core', swap)  6.3 us
    all_to_all x1, starting transfers between devices, exchange(): return lax.all_to_all(array, axes, split_axis=0, concat_axis=0, tiled=True)  3.94 us
    pallas_call x2, Pallas kernels, pick(): pl.pallas_call(functools.partial(pick_kernel, own), out_shape=pltpu.VMEM(...  2.46 us
  transfers between devices with their start and end apart: 3, of which 3 were waited for; matrix products, arithmetic and copies ran while one was open for 0% of the time, Pallas kernels for 9%

profile of v4, /device:TPU:1, one launch (start us, length us, event | category | flops | bytes accessed | tf_op | source)
XLA Modules:
  0.0 105.9 jit_solution(14840965941899946753)
XLA Ops:
  0.6 1.2 %other_half.1 = bf16[4,64,2048]{2,1,0:T(8,128)(2,1)S(1)} custom-call(bf16[64,4096]{1,0:T(8,128)(2,1)} %q_ref.5, bf16[64,4096]{1,0:T(8,128)(2,1)} %k_ref.5, bf16[64,4096]{1,0:T(8,128)(2,1)} %v_ref.5, bf16[64,4096]{1,0:T(8,128)(2,1)} %g_ref.5), custom_call_target="tpu_custom_call" | custom-call | bytes 2097152 | tf_op jit(solution)/shard_map/other_half/pallas_call | solution.py:58
  1.9 8.8 %collective-permute-start = (bf16[4,64,2048]{2,1,0:T(8,128)(2,1)S(1)}, bf16[4,64,2048]{2,1,0:T(8,128)(2,1)S(1)}, u32[]{:S(2)}, u32[]{:S(2)}) collective-permute-start(bf16[4,64,2048]{2,1,0:T(8,128)(2,1)S(1)} %other_half.1), channel_id=1, source_target_pairs={{0,1},{1,0},{2,3},{3,2},{4,5},{5,4},{6,7},{7,6},{8,9},{9,8},{10,11... | collective-permute-start | bytes 3145736 | tf_op jit(solution)/shard_map/ppermute | solution.py:347
  10.7 1.2 %own_half.1.own_ref = bf16[4,64,2048]{2,1,0:T(8,128)(2,1)S(1)} custom-call(bf16[64,4096]{1,0:T(8,128)(2,1)} %q_ref.5, bf16[64,4096]{1,0:T(8,128)(2,1)} %k_ref.5, bf16[64,4096]{1,0:T(8,128)(2,1)} %v_ref.5, bf16[64,4096]{1,0:T(8,128)(2,1)} %g_ref.5), custom_call_target="tpu_custom_call" | custom-call | bytes 2097152 | tf_op jit(solution)/shard_map/own_half/pallas_call | solution.py:58
  11.9 1.0 collective-permute-done.other_ref
  12.9 0.0 copy-start.2
  12.9 1.5 %chunk_states.1 = bf16[32,2,64,128]{3,2,1,0:T(8,128)(2,1)} custom-call(bf16[4,64,2048]{2,1,0:T(8,128)(2,1)S(1)} %own_half.1.own_ref, bf16[4,64,2048]{2,1,0:T(8,128)(2,1)S(1)} %collective-permute-done.other_ref), custom_call_target="tpu_custom_call" | custom-call | tf_op jit(solution)/shard_map/chunk_states/pallas_call | solution.py:106
  14.4 3.9 %all-to-all-start = ((bf16[32,2,64,128]{3,2,1,0:T(8,128)(2,1)}), bf16[32,2,64,128]{3,2,1,0:T(8,128)(2,1)S(1)}, u32[]{:S(2)}, u32[]{:S(2)}) async-start(bf16[32,2,64,128]{3,2,1,0:T(8,128)(2,1)} %chunk_states.1), calls=%async_computation | async-start | bytes 2097152 | tf_op jit(solution)/shard_map/all_to_all | solution.py:340
  18.3 0.0 copy-done.2
  18.4 6.5 %inner_part.1 = (f32[3,128,2048]{2,1,0:T(8,128)}, bf16[3,128,2048]{2,1,0:T(8,128)(2,1)}) custom-call(s32[1]{0:T(128)} %bitcast.core_ref, bf16[64,4096]{1,0:T(8,128)(2,1)} %q_ref.5, bf16[64,4096]{1,0:T(8,128)(2,1)} %k_ref.5, bf16[64,4096]{1,0:T(8,128)(2,1)} %v_ref.5, bf16[64,4096]{1,0:T(8,128)(2,1)} %g_ref.5, bf16[4,64,2048]{2,1,0:T(8,128)(2,1)} %copy-done.2), custom_call_target="tpu_custom_call" | custom-call | flops 335544320 | bytes 12582912 | tf_op jit(solution)/shard_map/inner_part/pallas_call | solution.py:237
  24.9 9.6 %all-to-all-done.near_ref = bf16[32,2,64,128]{3,2,1,0:T(8,128)(2,1)S(1)} async-done(((bf16[32,2,64,128]{3,2,1,0:T(8,128)(2,1)}), bf16[32,2,64,128]{3,2,1,0:T(8,128)(2,1)S(1)}, u32[]{:S(2)}, u32[]{:S(2)}) %all-to-all-start) | async-done | bytes 1048608 | tf_op jit(solution)/shard_map/all_to_all | solution.py:340
  34.4 0.0 copy-start
  34.4 0.0 copy-start.1
  34.4 0.1 group_total.1
  34.6 25.7 %all_to_all.20.far_ref = bf16[8,4,16,128]{3,2,1,0:T(8,128)(2,1)S(1)} all-to-all(bf16[8,4,16,128]{3,2,1,0:T(8,128)(2,1)S(1)} %group_total.1), channel_id=1, replica_groups=mesh['yf'=1,'yn'=4,'zh'=8,'zl'=2,'x'=4,'core'=2] {'yf','zh'}, dimensions={0} | all-to-all | bytes 262144 | tf_op jit(solution)/shard_map/all_to_all | solution.py:340
  60.3 15.6 %all_to_all.21.carry_ref = bf16[8,4,16,128]{3,2,1,0:T(8,128)(2,1)S(1)} all-to-all(bf16[8,4,16,128]{3,2,1,0:T(8,128)(2,1)S(1)} %group_carry.1), channel_id=1, replica_groups=mesh['yf'=1,'yn'=4,'zh'=8,'zl'=2,'x'=4,'core'=2] {'yf','zh'}, dimensions={0} | all-to-all | bytes 262144 | tf_op jit(solution)/shard_map/all_to_all | solution.py:340
  75.8 0.2 chip_carry.1
  76.0 19.9 %all_to_all.22.carry_ref = bf16[32,2,64,128]{3,2,1,0:T(8,128)(2,1)S(1)} all-to-all(bf16[32,2,64,128]{3,2,1,0:T(8,128)(2,1)S(1)} %chip_carry.1), channel_id=1, replica_groups=mesh['yf'=1,'yn'=4,'zh'=8,'zl'=2,'x'=4,'core'=2] {'yn','zl','x'}, dimensions={0} | all-to-all | bytes 2097152 | tf_op jit(solution)/shard_map/all_to_all | solution.py:340
  95.9 0.0 copy-done
  95.9 0.0 copy-done.1
  95.9 0.9 other_gradients.1
  96.8 6.3 %collective-permute-start.1 = (bf16[3,64,2048]{2,1,0:T(8,128)(2,1)S(1)}, bf16[3,64,2048]{2,1,0:T(8,128)(2,1)S(1)}, u32[]{:S(2)}, u32[]{:S(2)}) collective-permute-start(bf16[3,64,2048]{2,1,0:T(8,128)(2,1)S(1)} %other_gradients.1), channel_id=1, source_target_pairs={{0,1},{1,0},{2,3},{3,2},{4,5},{5,4},{6,7},{7,6},{8,9},{9,8},{10,11... | collective-permute-start | bytes 2359304 | tf_op jit(solution)/shard_map/ppermute | solution.py:353
  103.1 1.7 %own_gradients.1 = (bf16[64,4096]{1,0:T(8,128)(2,1)}, bf16[64,4096]{1,0:T(8,128)(2,1)}, bf16[64,4096]{1,0:T(8,128)(2,1)}) custom-call(f32[3,128,2048]{2,1,0:T(8,128)S(1)} %copy-done, bf16[3,128,2048]{2,1,0:T(8,128)(2,1)S(1)} %copy-done.1, bf16[32,2,64,128]{3,2,1,0:T(8,128)(2,1)S(1)} %all_to_all.22.carry_ref), custom_call_target="tpu_custom_call" | custom-call | flops 100663296 | bytes 4194304 | tf_op jit(solution)/shard_map/own_gradients/pallas_call | solution.py:305
  104.8 0.2 collective-permute-done.1.got_ref
  105.0 0.9 place_half.1
  (1 shorter events, 0.0 us)
Async XLA Ops:
  1.9 11.1 %collective-permute-start = (bf16[4,64,2048]{2,1,0:T(8,128)(2,1)S(1)}, bf16[4,64,2048]{2,1,0:T(8,128)(2,1)S(1)}, u32[]{:S(2)}, u32[]{:S(2)}) collective-permute-start(bf16[4,64,2048]{2,1,0:T(8,128)(2,1)S(1)} %other_half.1), channel_id=1, source_target_pairs={{0,1},{1,0},{2,3},{3,2},{4,5},{5,4},{6,7},{7,6},{8,9},{9,8},{10,11... | collective-permute-start | bytes 3145736 | tf_op jit(solution)/shard_map/ppermute | solution.py:347
  12.9 5.4 %copy-start.2 = (bf16[4,64,2048]{2,1,0:T(8,128)(2,1)}, bf16[4,64,2048]{2,1,0:T(8,128)(2,1)S(1)}, u32[]{:S(2)}) copy-start(bf16[4,64,2048]{2,1,0:T(8,128)(2,1)S(1)} %collective-permute-done.other_ref) | copy-start | bytes 3145732
  14.4 20.0 %all-to-all-start = ((bf16[32,2,64,128]{3,2,1,0:T(8,128)(2,1)}), bf16[32,2,64,128]{3,2,1,0:T(8,128)(2,1)S(1)}, u32[]{:S(2)}, u32[]{:S(2)}) async-start(bf16[32,2,64,128]{3,2,1,0:T(8,128)(2,1)} %chunk_states.1), calls=%async_computation | async-start | bytes 2097152 | tf_op jit(solution)/shard_map/all_to_all | solution.py:340
  34.4 61.5 %copy-start = (f32[3,128,2048]{2,1,0:T(8,128)S(1)}, f32[3,128,2048]{2,1,0:T(8,128)}, u32[]{:S(2)}) copy-start(f32[3,128,2048]{2,1,0:T(8,128)} %get-tuple-element.13.inner_ref) | copy-start | bytes 9437188
  34.4 61.5 %copy-start.1 = (bf16[3,128,2048]{2,1,0:T(8,128)(2,1)S(1)}, bf16[3,128,2048]{2,1,0:T(8,128)(2,1)}, u32[]{:S(2)}) copy-start(bf16[3,128,2048]{2,1,0:T(8,128)(2,1)} %get-tuple-element.14.kept_ref) | copy-start | bytes 4718596
  96.8 8.2 %collective-permute-start.1 = (bf16[3,64,2048]{2,1,0:T(8,128)(2,1)S(1)}, bf16[3,64,2048]{2,1,0:T(8,128)(2,1)S(1)}, u32[]{:S(2)}, u32[]{:S(2)}) collective-permute-start(bf16[3,64,2048]{2,1,0:T(8,128)(2,1)S(1)} %other_gradients.1), channel_id=1, source_target_pairs={{0,1},{1,0},{2,3},{3,2},{4,5},{5,4},{6,7},{7,6},{8,9},{9,8},{10,11... | collective-permute-start | bytes 2359304 | tf_op jit(solution)/shard_map/ppermute | solution.py:353

commit v5 on v4

--- a/solution.py
+++ b/solution.py
@@ -17,7 +17,7 @@
 STEPS = 4
 STEP_HEADS = HALF_HEADS // STEPS
 F32, BF16 = jnp.float32, jnp.bfloat16
-NEAR_AXES, FAR_AXES = ("yn", "zl", "x"), ("yf", "zh")
+NEAR_AXES, FAR_AXES = ("zl", "x", "yn"), ("yf", "zh")
 BAND = 64
 SMALL, LARGE = 32 * 1024 * 1024, 60 * 1024 * 1024
 
@@ -128,12 +128,21 @@
     return own, other
 
 
+def member(span, chip):
+    place = {"yn": span, "zl": chip // 4, "x": chip % 4}
+    sizes = {"yn": NEAR_Y, "zl": 2, "x": 4}
+    index = 0
+    for axis in NEAR_AXES:
+        index = index * sizes[axis] + place[axis]
+    return index
+
+
 def total_kernel(near_ref, out_ref):
     half = FAR // 2
     for span in range(NEAR_Y):
-        total = near_ref[span * CHIPS].astype(F32)
+        total = near_ref[member(span, 0)].astype(F32)
         for chip in range(1, CHIPS):
-            total += near_ref[span * CHIPS + chip].astype(F32)
+            total += near_ref[member(span, chip)].astype(F32)
         total = total.astype(BF16)
         for slot in range(FAR):
             block = slot % half * BLOCK
@@ -194,8 +203,8 @@
         for i, order in enumerate((range(CHIPS), range(CHIPS)[::-1])):
             total = jnp.concatenate([carry_ref[i * half + j, span] for j in range(half)], axis=0).astype(F32)
             for chip in order:
-                out_ref[span * CHIPS + chip, i] = total.astype(BF16)
-                total += near_ref[span * CHIPS + chip, i].astype(F32)
+                out_ref[member(span, chip), i] = total.astype(BF16)
+                total += near_ref[member(span, chip), i].astype(F32)
 
 
 def chip_carry(near, carry):

time: 106 us -> 105 us (level)
  blocking collectives: 61.1 us -> 59.8 us
    all_to_all x3, blocking collectives: 61.1 us -> 59.8 us  [exchange(): return lax.all_to_all(array, axes, split_axis=0, concat_axis=0, tiled=True)]
where the time goes in v5:
time: 105 us
  blocking collectives  59.8 us (57%)
  starting transfers between devices  19.8 us (19%)
  Pallas kernels  14.3 us (14%)
  waiting for transfers between devices  10.1 us (10%)
    all_to_all x3, blocking collectives, exchange(): return lax.all_to_all(array, axes, split_axis=0, concat_axis=0, tiled=True)  59.8 us
    all_to_all x1, waiting for transfers between devices, exchange(): return lax.all_to_all(array, axes, split_axis=0, concat_axis=0, tiled=True)  8.85 us
    ppermute x1, starting transfers between devices, local(): other = lax.ppermute(pick(arrays, False), 'core', swap)  8.79 us
    ppermute x1, starting transfers between devices, local(): got = lax.ppermute(other_gradients(*inner, carry), 'core', swap)  7.07 us
    pallas_call x1, Pallas kernels, inner_part(): pl.pallas_call(inner_kernel, out_shape=[pltpu.HBM((3, 2 * rows, width //...  6.52 us
    all_to_all x1, starting transfers between devices, exchange(): return lax.all_to_all(array, axes, split_axis=0, concat_axis=0, tiled=True)  3.94 us
    pallas_call x2, Pallas kernels, pick(): pl.pallas_call(functools.partial(pick_kernel, own), out_shape=pltpu.VMEM(...  2.46 us
  transfers between devices with their start and end apart: 3, of which 3 were waited for; matrix products, arithmetic and copies ran while one was open for 0% of the time, Pallas kernels for 9%

profile of v5, /device:TPU:1, one launch (start us, length us, event | category | flops | bytes accessed | tf_op | source)
XLA Modules:
  0.0 104.6 jit_solution(7142138659366421390)
XLA Ops:
  0.6 1.2 %other_half.1 = bf16[4,64,2048]{2,1,0:T(8,128)(2,1)S(1)} custom-call(bf16[64,4096]{1,0:T(8,128)(2,1)} %q_ref.5, bf16[64,4096]{1,0:T(8,128)(2,1)} %k_ref.5, bf16[64,4096]{1,0:T(8,128)(2,1)} %v_ref.5, bf16[64,4096]{1,0:T(8,128)(2,1)} %g_ref.5), custom_call_target="tpu_custom_call" | custom-call | bytes 2097152 | tf_op jit(solution)/shard_map/other_half/pallas_call | solution.py:58
  1.9 8.8 %collective-permute-start = (bf16[4,64,2048]{2,1,0:T(8,128)(2,1)S(1)}, bf16[4,64,2048]{2,1,0:T(8,128)(2,1)S(1)}, u32[]{:S(2)}, u32[]{:S(2)}) collective-permute-start(bf16[4,64,2048]{2,1,0:T(8,128)(2,1)S(1)} %other_half.1), channel_id=1, source_target_pairs={{0,1},{1,0},{2,3},{3,2},{4,5},{5,4},{6,7},{7,6},{8,9},{9,8},{10,11... | collective-permute-start | bytes 3145736 | tf_op jit(solution)/shard_map/ppermute | solution.py:356
  10.7 1.2 %own_half.1.own_ref = bf16[4,64,2048]{2,1,0:T(8,128)(2,1)S(1)} custom-call(bf16[64,4096]{1,0:T(8,128)(2,1)} %q_ref.5, bf16[64,4096]{1,0:T(8,128)(2,1)} %k_ref.5, bf16[64,4096]{1,0:T(8,128)(2,1)} %v_ref.5, bf16[64,4096]{1,0:T(8,128)(2,1)} %g_ref.5), custom_call_target="tpu_custom_call" | custom-call | bytes 2097152 | tf_op jit(solution)/shard_map/own_half/pallas_call | solution.py:58
  11.9 1.0 collective-permute-done.other_ref
  12.9 0.0 copy-start.2
  12.9 1.5 %chunk_states.1 = bf16[32,2,64,128]{3,2,1,0:T(8,128)(2,1)} custom-call(bf16[4,64,2048]{2,1,0:T(8,128)(2,1)S(1)} %own_half.1.own_ref, bf16[4,64,2048]{2,1,0:T(8,128)(2,1)S(1)} %collective-permute-done.other_ref), custom_call_target="tpu_custom_call" | custom-call | tf_op jit(solution)/shard_map/chunk_states/pallas_call | solution.py:106
  14.4 3.9 %all-to-all-start = ((bf16[32,2,64,128]{3,2,1,0:T(8,128)(2,1)}), bf16[32,2,64,128]{3,2,1,0:T(8,128)(2,1)S(1)}, u32[]{:S(2)}, u32[]{:S(2)}) async-start(bf16[32,2,64,128]{3,2,1,0:T(8,128)(2,1)} %chunk_states.1), calls=%async_computation | async-start | bytes 2097152 | tf_op jit(solution)/shard_map/all_to_all | solution.py:349
  18.3 0.0 copy-done.2
  18.4 6.5 %inner_part.1 = (f32[3,128,2048]{2,1,0:T(8,128)}, bf16[3,128,2048]{2,1,0:T(8,128)(2,1)}) custom-call(s32[1]{0:T(128)} %bitcast.core_ref, bf16[64,4096]{1,0:T(8,128)(2,1)} %q_ref.5, bf16[64,4096]{1,0:T(8,128)(2,1)} %k_ref.5, bf16[64,4096]{1,0:T(8,128)(2,1)} %v_ref.5, bf16[64,4096]{1,0:T(8,128)(2,1)} %g_ref.5, bf16[4,64,2048]{2,1,0:T(8,128)(2,1)} %copy-done.2), custom_call_target="tpu_custom_call" | custom-call | flops 335544320 | bytes 12582912 | tf_op jit(solution)/shard_map/inner_part/pallas_call | solution.py:246
  24.9 8.8 %all-to-all-done.near_ref = bf16[32,2,64,128]{3,2,1,0:T(8,128)(2,1)S(1)} async-done(((bf16[32,2,64,128]{3,2,1,0:T(8,128)(2,1)}), bf16[32,2,64,128]{3,2,1,0:T(8,128)(2,1)S(1)}, u32[]{:S(2)}, u32[]{:S(2)}) %all-to-all-start) | async-done | bytes 1048608 | tf_op jit(solution)/shard_map/all_to_all | solution.py:349
  33.7 0.0 copy-start
  33.7 0.0 copy-start.1
  33.7 0.1 group_total.1
  33.9 26.6 %all_to_all.20.far_ref = bf16[8,4,16,128]{3,2,1,0:T(8,128)(2,1)S(1)} all-to-all(bf16[8,4,16,128]{3,2,1,0:T(8,128)(2,1)S(1)} %group_total.1), channel_id=1, replica_groups=mesh['yf'=1,'yn'=4,'zh'=8,'zl'=2,'x'=4,'core'=2] {'yf','zh'}, dimensions={0} | all-to-all | bytes 262144 | tf_op jit(solution)/shard_map/all_to_all | solution.py:349
  60.5 16.1 %all_to_all.21.carry_ref = bf16[8,4,16,128]{3,2,1,0:T(8,128)(2,1)S(1)} all-to-all(bf16[8,4,16,128]{3,2,1,0:T(8,128)(2,1)S(1)} %group_carry.1), channel_id=1, replica_groups=mesh['yf'=1,'yn'=4,'zh'=8,'zl'=2,'x'=4,'core'=2] {'yf','zh'}, dimensions={0} | all-to-all | bytes 262144 | tf_op jit(solution)/shard_map/all_to_all | solution.py:349
  76.6 0.2 chip_carry.1
  76.8 17.1 %all_to_all.22.carry_ref = bf16[32,2,64,128]{3,2,1,0:T(8,128)(2,1)S(1)} all-to-all(bf16[32,2,64,128]{3,2,1,0:T(8,128)(2,1)S(1)} %chip_carry.1), channel_id=1, replica_groups=mesh['yf'=1,'yn'=4,'zh'=8,'zl'=2,'x'=4,'core'=2] {'zl','x','yn'}, dimensions={0} | all-to-all | bytes 2097152 | tf_op jit(solution)/shard_map/all_to_all | solution.py:349
  93.9 0.0 copy-done
  93.9 0.0 copy-done.1
  93.9 0.9 other_gradients.1
  94.8 7.1 %collective-permute-start.1 = (bf16[3,64,2048]{2,1,0:T(8,128)(2,1)S(1)}, bf16[3,64,2048]{2,1,0:T(8,128)(2,1)S(1)}, u32[]{:S(2)}, u32[]{:S(2)}) collective-permute-start(bf16[3,64,2048]{2,1,0:T(8,128)(2,1)S(1)} %other_gradients.1), channel_id=1, source_target_pairs={{0,1},{1,0},{2,3},{3,2},{4,5},{5,4},{6,7},{7,6},{8,9},{9,8},{10,11... | collective-permute-start | bytes 2359304 | tf_op jit(solution)/shard_map/ppermute | solution.py:362
  101.9 1.7 %own_gradients.1 = (bf16[64,4096]{1,0:T(8,128)(2,1)}, bf16[64,4096]{1,0:T(8,128)(2,1)}, bf16[64,4096]{1,0:T(8,128)(2,1)}) custom-call(f32[3,128,2048]{2,1,0:T(8,128)S(1)} %copy-done, bf16[3,128,2048]{2,1,0:T(8,128)(2,1)S(1)} %copy-done.1, bf16[32,2,64,128]{3,2,1,0:T(8,128)(2,1)S(1)} %all_to_all.22.carry_ref), custom_call_target="tpu_custom_call" | custom-call | flops 100663296 | bytes 4194304 | tf_op jit(solution)/shard_map/own_gradients/pallas_call | solution.py:314
  103.5 0.2 collective-permute-done.1.got_ref
  103.7 0.9 place_half.1
  (1 shorter events, 0.0 us)
Async XLA Ops:
  1.9 11.1 %collective-permute-start = (bf16[4,64,2048]{2,1,0:T(8,128)(2,1)S(1)}, bf16[4,64,2048]{2,1,0:T(8,128)(2,1)S(1)}, u32[]{:S(2)}, u32[]{:S(2)}) collective-permute-start(bf16[4,64,2048]{2,1,0:T(8,128)(2,1)S(1)} %other_half.1), channel_id=1, source_target_pairs={{0,1},{1,0},{2,3},{3,2},{4,5},{5,4},{6,7},{7,6},{8,9},{9,8},{10,11... | collective-permute-start | bytes 3145736 | tf_op jit(solution)/shard_map/ppermute | solution.py:356
  12.9 5.4 %copy-start.2 = (bf16[4,64,2048]{2,1,0:T(8,128)(2,1)}, bf16[4,64,2048]{2,1,0:T(8,128)(2,1)S(1)}, u32[]{:S(2)}) copy-start(bf16[4,64,2048]{2,1,0:T(8,128)(2,1)S(1)} %collective-permute-done.other_ref) | copy-start | bytes 3145732
  14.4 19.3 %all-to-all-start = ((bf16[32,2,64,128]{3,2,1,0:T(8,128)(2,1)}), bf16[32,2,64,128]{3,2,1,0:T(8,128)(2,1)S(1)}, u32[]{:S(2)}, u32[]{:S(2)}) async-start(bf16[32,2,64,128]{3,2,1,0:T(8,128)(2,1)} %chunk_states.1), calls=%async_computation | async-start | bytes 2097152 | tf_op jit(solution)/shard_map/all_to_all | solution.py:349
  33.7 60.1 %copy-start = (f32[3,128,2048]{2,1,0:T(8,128)S(1)}, f32[3,128,2048]{2,1,0:T(8,128)}, u32[]{:S(2)}) copy-start(f32[3,128,2048]{2,1,0:T(8,128)} %get-tuple-element.13.inner_ref) | copy-start | bytes 9437188
  33.7 60.1 %copy-start.1 = (bf16[3,128,2048]{2,1,0:T(8,128)(2,1)S(1)}, bf16[3,128,2048]{2,1,0:T(8,128)(2,1)}, u32[]{:S(2)}) copy-start(bf16[3,128,2048]{2,1,0:T(8,128)(2,1)} %get-tuple-element.14.kept_ref) | copy-start | bytes 4718596
  94.8 9.0 %collective-permute-start.1 = (bf16[3,64,2048]{2,1,0:T(8,128)(2,1)S(1)}, bf16[3,64,2048]{2,1,0:T(8,128)(2,1)S(1)}, u32[]{:S(2)}, u32[]{:S(2)}) collective-permute-start(bf16[3,64,2048]{2,1,0:T(8,128)(2,1)S(1)} %other_gradients.1), channel_id=1, source_target_pairs={{0,1},{1,0},{2,3},{3,2},{4,5},{5,4},{6,7},{7,6},{8,9},{9,8},{10,11... | collective-permute-start | bytes 2359304 | tf_op jit(solution)/shard_map/ppermute | solution.py:362

commit v6 on v5

--- a/solution.py
+++ b/solution.py
@@ -17,7 +17,7 @@
 STEPS = 4
 STEP_HEADS = HALF_HEADS // STEPS
 F32, BF16 = jnp.float32, jnp.bfloat16
-NEAR_AXES, FAR_AXES = ("zl", "x", "yn"), ("yf", "zh")
+NEAR_AXES, FAR_AXES = ("zl", "x", "yn"), ("yf", "zc", "zb", "za")
 BAND = 64
 SMALL, LARGE = 32 * 1024 * 1024, 60 * 1024 * 1024
 
@@ -164,7 +164,7 @@
     order = []
     for y in range(SPANS_Y):
         far_at, near_at = divmod(y, NEAR_Y)
-        order += [(far_at * FAR_Z + z, near_at) for z in range(FAR_Z)]
+        order += [(far_at * FAR_Z + z % 2 * 4 + z // 2 % 2 * 2 + z // 4, near_at) for z in range(FAR_Z)]
     return order
 
 
@@ -364,7 +364,7 @@
 
 
 def solution(mesh):
-    sizes = {"yf": SPANS_Y // NEAR_Y, "yn": NEAR_Y, "zh": FAR_Z, "zl": 2, "x": 4, "core": CORES}
+    sizes = {"yf": SPANS_Y // NEAR_Y, "yn": NEAR_Y, "za": 2, "zb": 2, "zc": 2, "zl": 2, "x": 4, "core": CORES}
     names = tuple(sizes)
     chips = Mesh(mesh.devices.reshape(tuple(sizes.values())), names)
     rows = P(names, None)

time: 105 us -> 105 us (level)
  no operation moved by 1% of the time
where the time goes in v6:
time: 105 us; the launch traced here: 104 us
  blocking collectives  59.2 us (56%)
  starting transfers between devices  19.8 us (19%)
  Pallas kernels  14.3 us (14%)
  waiting for transfers between devices  10.1 us (10%)
    all_to_all x3, blocking collectives, exchange(): return lax.all_to_all(array, axes, split_axis=0, concat_axis=0, tiled=True)  59.2 us
    all_to_all x1, waiting for transfers between devices, exchange(): return lax.all_to_all(array, axes, split_axis=0, concat_axis=0, tiled=True)  8.85 us
    ppermute x1, starting transfers between devices, local(): other = lax.ppermute(pick(arrays, False), 'core', swap)  8.79 us
    ppermute x1, starting transfers between devices, local(): got = lax.ppermute(other_gradients(*inner, carry), 'core', swap)  7.11 us
    pallas_call x1, Pallas kernels, inner_part(): pl.pallas_call(inner_kernel, out_shape=[pltpu.HBM((3, 2 * rows, width //...  6.52 us
    all_to_all x1, starting transfers between devices, exchange(): return lax.all_to_all(array, axes, split_axis=0, concat_axis=0, tiled=True)  3.94 us
    pallas_call x2, Pallas kernels, pick(): pl.pallas_call(functools.partial(pick_kernel, own), out_shape=pltpu.VMEM(...  2.46 us
  transfers between devices with their start and end apart: 3, of which 3 were waited for; matrix products, arithmetic and copies ran while one was open for 0% of the time, Pallas kernels for 9%

profile of v6, /device:TPU:1, one launch (start us, length us, event | category | flops | bytes accessed | tf_op | source)
XLA Modules:
  0.0 104.1 jit_solution(7590786221118002685)
XLA Ops:
  0.6 1.2 %other_half.1 = bf16[4,64,2048]{2,1,0:T(8,128)(2,1)S(1)} custom-call(bf16[64,4096]{1,0:T(8,128)(2,1)} %q_ref.5, bf16[64,4096]{1,0:T(8,128)(2,1)} %k_ref.5, bf16[64,4096]{1,0:T(8,128)(2,1)} %v_ref.5, bf16[64,4096]{1,0:T(8,128)(2,1)} %g_ref.5), custom_call_target="tpu_custom_call" | custom-call | bytes 2097152 | tf_op jit(solution)/shard_map/other_half/pallas_call | solution.py:58
  1.9 8.8 %collective-permute-start = (bf16[4,64,2048]{2,1,0:T(8,128)(2,1)S(1)}, bf16[4,64,2048]{2,1,0:T(8,128)(2,1)S(1)}, u32[]{:S(2)}, u32[]{:S(2)}) collective-permute-start(bf16[4,64,2048]{2,1,0:T(8,128)(2,1)S(1)} %other_half.1), channel_id=1, source_target_pairs={{0,1},{1,0},{2,3},{3,2},{4,5},{5,4},{6,7},{7,6},{8,9},{9,8},{10,11... | collective-permute-start | bytes 3145736 | tf_op jit(solution)/shard_map/ppermute | solution.py:356
  10.7 1.2 %own_half.1.own_ref = bf16[4,64,2048]{2,1,0:T(8,128)(2,1)S(1)} custom-call(bf16[64,4096]{1,0:T(8,128)(2,1)} %q_ref.5, bf16[64,4096]{1,0:T(8,128)(2,1)} %k_ref.5, bf16[64,4096]{1,0:T(8,128)(2,1)} %v_ref.5, bf16[64,4096]{1,0:T(8,128)(2,1)} %g_ref.5), custom_call_target="tpu_custom_call" | custom-call | bytes 2097152 | tf_op jit(solution)/shard_map/own_half/pallas_call | solution.py:58
  11.9 1.0 collective-permute-done.other_ref
  12.9 0.0 copy-start.2
  12.9 1.5 %chunk_states.1 = bf16[32,2,64,128]{3,2,1,0:T(8,128)(2,1)} custom-call(bf16[4,64,2048]{2,1,0:T(8,128)(2,1)S(1)} %own_half.1.own_ref, bf16[4,64,2048]{2,1,0:T(8,128)(2,1)S(1)} %collective-permute-done.other_ref), custom_call_target="tpu_custom_call" | custom-call | tf_op jit(solution)/shard_map/chunk_states/pallas_call | solution.py:106
  14.4 3.9 %all-to-all-start = ((bf16[32,2,64,128]{3,2,1,0:T(8,128)(2,1)}), bf16[32,2,64,128]{3,2,1,0:T(8,128)(2,1)S(1)}, u32[]{:S(2)}, u32[]{:S(2)}) async-start(bf16[32,2,64,128]{3,2,1,0:T(8,128)(2,1)} %chunk_states.1), calls=%async_computation | async-start | bytes 2097152 | tf_op jit(solution)/shard_map/all_to_all | solution.py:349
  18.3 0.0 copy-done.2
  18.4 6.5 %inner_part.1 = (f32[3,128,2048]{2,1,0:T(8,128)}, bf16[3,128,2048]{2,1,0:T(8,128)(2,1)}) custom-call(s32[1]{0:T(128)} %bitcast.core_ref, bf16[64,4096]{1,0:T(8,128)(2,1)} %q_ref.5, bf16[64,4096]{1,0:T(8,128)(2,1)} %k_ref.5, bf16[64,4096]{1,0:T(8,128)(2,1)} %v_ref.5, bf16[64,4096]{1,0:T(8,128)(2,1)} %g_ref.5, bf16[4,64,2048]{2,1,0:T(8,128)(2,1)} %copy-done.2), custom_call_target="tpu_custom_call" | custom-call | flops 335544320 | bytes 12582912 | tf_op jit(solution)/shard_map/inner_part/pallas_call | solution.py:246
  24.9 8.8 %all-to-all-done.near_ref = bf16[32,2,64,128]{3,2,1,0:T(8,128)(2,1)S(1)} async-done(((bf16[32,2,64,128]{3,2,1,0:T(8,128)(2,1)}), bf16[32,2,64,128]{3,2,1,0:T(8,128)(2,1)S(1)}, u32[]{:S(2)}, u32[]{:S(2)}) %all-to-all-start) | async-done | bytes 1048608 | tf_op jit(solution)/shard_map/all_to_all | solution.py:349
  33.7 0.0 copy-start
  33.7 0.0 copy-start.1
  33.7 0.1 group_total.1
  33.9 24.8 %all_to_all.20.far_ref = bf16[8,4,16,128]{3,2,1,0:T(8,128)(2,1)S(1)} all-to-all(bf16[8,4,16,128]{3,2,1,0:T(8,128)(2,1)S(1)} %group_total.1), channel_id=1, replica_groups=mesh['yf'=1,'yn'=4,'za'=2,'zb'=2,'zc'=2,'zl'=2,'x'=4,'core'=2] {'yf','zc..., dimensions={0} | all-to-all | bytes 262144 | tf_op jit(solution)/shard_map/all_to_all | solution.py:349
  58.7 15.8 %all_to_all.21.carry_ref = bf16[8,4,16,128]{3,2,1,0:T(8,128)(2,1)S(1)} all-to-all(bf16[8,4,16,128]{3,2,1,0:T(8,128)(2,1)S(1)} %group_carry.1), channel_id=1, replica_groups=mesh['yf'=1,'yn'=4,'za'=2,'zb'=2,'zc'=2,'zl'=2,'x'=4,'core'=2] {'yf','zc..., dimensions={0} | all-to-all | bytes 262144 | tf_op jit(solution)/shard_map/all_to_all | solution.py:349
  74.5 0.2 chip_carry.1
  74.7 18.6 %all_to_all.22.carry_ref = bf16[32,2,64,128]{3,2,1,0:T(8,128)(2,1)S(1)} all-to-all(bf16[32,2,64,128]{3,2,1,0:T(8,128)(2,1)S(1)} %chip_carry.1), channel_id=1, replica_groups=mesh['yf'=1,'yn'=4,'za'=2,'zb'=2,'zc'=2,'zl'=2,'x'=4,'core'=2] {'zl','x'..., dimensions={0} | all-to-all | bytes 2097152 | tf_op jit(solution)/shard_map/all_to_all | solution.py:349
  93.3 0.0 copy-done
  93.3 0.0 copy-done.1
  93.3 0.9 other_gradients.1
  94.2 7.1 %collective-permute-start.1 = (bf16[3,64,2048]{2,1,0:T(8,128)(2,1)S(1)}, bf16[3,64,2048]{2,1,0:T(8,128)(2,1)S(1)}, u32[]{:S(2)}, u32[]{:S(2)}) collective-permute-start(bf16[3,64,2048]{2,1,0:T(8,128)(2,1)S(1)} %other_gradients.1), channel_id=1, source_target_pairs={{0,1},{1,0},{2,3},{3,2},{4,5},{5,4},{6,7},{7,6},{8,9},{9,8},{10,11... | collective-permute-start | bytes 2359304 | tf_op jit(solution)/shard_map/ppermute | solution.py:362
  101.3 1.7 %own_gradients.1 = (bf16[64,4096]{1,0:T(8,128)(2,1)}, bf16[64,4096]{1,0:T(8,128)(2,1)}, bf16[64,4096]{1,0:T(8,128)(2,1)}) custom-call(f32[3,128,2048]{2,1,0:T(8,128)S(1)} %copy-done, bf16[3,128,2048]{2,1,0:T(8,128)(2,1)S(1)} %copy-done.1, bf16[32,2,64,128]{3,2,1,0:T(8,128)(2,1)S(1)} %all_to_all.22.carry_ref), custom_call_target="tpu_custom_call" | custom-call | flops 100663296 | bytes 4194304 | tf_op jit(solution)/shard_map/own_gradients/pallas_call | solution.py:314
  103.0 0.2 collective-permute-done.1.got_ref
  103.2 0.9 place_half.1
  (1 shorter events, 0.0 us)
Async XLA Ops:
  1.9 11.1 %collective-permute-start = (bf16[4,64,2048]{2,1,0:T(8,128)(2,1)S(1)}, bf16[4,64,2048]{2,1,0:T(8,128)(2,1)S(1)}, u32[]{:S(2)}, u32[]{:S(2)}) collective-permute-start(bf16[4,64,2048]{2,1,0:T(8,128)(2,1)S(1)} %other_half.1), channel_id=1, source_target_pairs={{0,1},{1,0},{2,3},{3,2},{4,5},{5,4},{6,7},{7,6},{8,9},{9,8},{10,11... | collective-permute-start | bytes 3145736 | tf_op jit(solution)/shard_map/ppermute | solution.py:356
  12.9 5.4 %copy-start.2 = (bf16[4,64,2048]{2,1,0:T(8,128)(2,1)}, bf16[4,64,2048]{2,1,0:T(8,128)(2,1)S(1)}, u32[]{:S(2)}) copy-start(bf16[4,64,2048]{2,1,0:T(8,128)(2,1)S(1)} %collective-permute-done.other_ref) | copy-start | bytes 3145732
  14.4 19.3 %all-to-all-start = ((bf16[32,2,64,128]{3,2,1,0:T(8,128)(2,1)}), bf16[32,2,64,128]{3,2,1,0:T(8,128)(2,1)S(1)}, u32[]{:S(2)}, u32[]{:S(2)}) async-start(bf16[32,2,64,128]{3,2,1,0:T(8,128)(2,1)} %chunk_states.1), calls=%async_computation | async-start | bytes 2097152 | tf_op jit(solution)/shard_map/all_to_all | solution.py:349
  33.7 59.5 %copy-start = (f32[3,128,2048]{2,1,0:T(8,128)S(1)}, f32[3,128,2048]{2,1,0:T(8,128)}, u32[]{:S(2)}) copy-start(f32[3,128,2048]{2,1,0:T(8,128)} %get-tuple-element.13.inner_ref) | copy-start | bytes 9437188
  33.7 59.5 %copy-start.1 = (bf16[3,128,2048]{2,1,0:T(8,128)(2,1)S(1)}, bf16[3,128,2048]{2,1,0:T(8,128)(2,1)}, u32[]{:S(2)}) copy-start(bf16[3,128,2048]{2,1,0:T(8,128)(2,1)} %get-tuple-element.14.kept_ref) | copy-start | bytes 4718596
  94.2 9.0 %collective-permute-start.1 = (bf16[3,64,2048]{2,1,0:T(8,128)(2,1)S(1)}, bf16[3,64,2048]{2,1,0:T(8,128)(2,1)S(1)}, u32[]{:S(2)}, u32[]{:S(2)}) collective-permute-start(bf16[3,64,2048]{2,1,0:T(8,128)(2,1)S(1)} %other_gradients.1), channel_id=1, source_target_pairs={{0,1},{1,0},{2,3},{3,2},{4,5},{5,4},{6,7},{7,6},{8,9},{9,8},{10,11... | collective-permute-start | bytes 2359304 | tf_op jit(solution)/shard_map/ppermute | solution.py:362

commit v7 on v6

--- a/solution.py
+++ b/solution.py
@@ -17,7 +17,7 @@
 STEPS = 4
 STEP_HEADS = HALF_HEADS // STEPS
 F32, BF16 = jnp.float32, jnp.bfloat16
-NEAR_AXES, FAR_AXES = ("zl", "x", "yn"), ("yf", "zc", "zb", "za")
+NEAR_AXES, FAR_AXES = ("zl", "x", "yl", "yh"), ("yf", "zc", "zb", "za")
 BAND = 64
 SMALL, LARGE = 32 * 1024 * 1024, 60 * 1024 * 1024
 
@@ -129,8 +129,8 @@
 
 
 def member(span, chip):
-    place = {"yn": span, "zl": chip // 4, "x": chip % 4}
-    sizes = {"yn": NEAR_Y, "zl": 2, "x": 4}
+    place = {"yh": span // 2, "yl": span % 2, "zl": chip // 4, "x": chip % 4}
+    sizes = {"yh": 2, "yl": 2, "zl": 2, "x": 4}
     index = 0
     for axis in NEAR_AXES:
         index = index * sizes[axis] + place[axis]
@@ -364,7 +364,7 @@
 
 
 def solution(mesh):
-    sizes = {"yf": SPANS_Y // NEAR_Y, "yn": NEAR_Y, "za": 2, "zb": 2, "zc": 2, "zl": 2, "x": 4, "core": CORES}
+    sizes = {"yf": SPANS_Y // NEAR_Y, "yh": 2, "yl": 2, "za": 2, "zb": 2, "zc": 2, "zl": 2, "x": 4, "core": CORES}
     names = tuple(sizes)
     chips = Mesh(mesh.devices.reshape(tuple(sizes.values())), names)
     rows = P(names, None)

time: 105 us -> 106 us (level)
  waiting for transfers between devices: 10.1 us -> 11.3 us
    all_to_all x1, waiting for transfers between devices: 8.85 us -> 10.1 us  [exchange(): return lax.all_to_all(array, axes, split_axis=0, concat_axis=0, tiled=True)]
where the time goes in v7:
time: 106 us; the launch traced here: 105 us
  blocking collectives  59.3 us (56%)
  starting transfers between devices  19.8 us (19%)
  Pallas kernels  14.3 us (13%)
  waiting for transfers between devices  11.3 us (11%)
    all_to_all x3, blocking collectives, exchange(): return lax.all_to_all(array, axes, split_axis=0, concat_axis=0, tiled=True)  59.3 us
    all_to_all x1, waiting for transfers between devices, exchange(): return lax.all_to_all(array, axes, split_axis=0, concat_axis=0, tiled=True)  10.1 us
    ppermute x1, starting transfers between devices, local(): other = lax.ppermute(pick(arrays, False), 'core', swap)  8.79 us
    ppermute x1, starting transfers between devices, local(): got = lax.ppermute(other_gradients(*inner, carry), 'core', swap)  7.04 us
    pallas_call x1, Pallas kernels, inner_part(): pl.pallas_call(inner_kernel, out_shape=[pltpu.HBM((3, 2 * rows, width //...  6.52 us
    all_to_all x1, starting transfers between devices, exchange(): return lax.all_to_all(array, axes, split_axis=0, concat_axis=0, tiled=True)  3.94 us
    pallas_call x2, Pallas kernels, pick(): pl.pallas_call(functools.partial(pick_kernel, own), out_shape=pltpu.VMEM(...  2.46 us
  transfers between devices with their start and end apart: 3, of which 3 were waited for; matrix products, arithmetic and copies ran while one was open for 0% of the time, Pallas kernels for 9%

profile of v7, /device:TPU:1, one launch (start us, length us, event | category | flops | bytes accessed | tf_op | source)
XLA Modules:
  0.0 105.4 jit_solution(8749489054386802591)
XLA Ops:
  0.6 1.2 %other_half.1 = bf16[4,64,2048]{2,1,0:T(8,128)(2,1)S(1)} custom-call(bf16[64,4096]{1,0:T(8,128)(2,1)} %q_ref.5, bf16[64,4096]{1,0:T(8,128)(2,1)} %k_ref.5, bf16[64,4096]{1,0:T(8,128)(2,1)} %v_ref.5, bf16[64,4096]{1,0:T(8,128)(2,1)} %g_ref.5), custom_call_target="tpu_custom_call" | custom-call | bytes 2097152 | tf_op jit(solution)/shard_map/other_half/pallas_call | solution.py:58
  1.9 8.8 %collective-permute-start = (bf16[4,64,2048]{2,1,0:T(8,128)(2,1)S(1)}, bf16[4,64,2048]{2,1,0:T(8,128)(2,1)S(1)}, u32[]{:S(2)}, u32[]{:S(2)}) collective-permute-start(bf16[4,64,2048]{2,1,0:T(8,128)(2,1)S(1)} %other_half.1), channel_id=1, source_target_pairs={{0,1},{1,0},{2,3},{3,2},{4,5},{5,4},{6,7},{7,6},{8,9},{9,8},{10,11... | collective-permute-start | bytes 3145736 | tf_op jit(solution)/shard_map/ppermute | solution.py:356
  10.7 1.2 %own_half.1.own_ref = bf16[4,64,2048]{2,1,0:T(8,128)(2,1)S(1)} custom-call(bf16[64,4096]{1,0:T(8,128)(2,1)} %q_ref.5, bf16[64,4096]{1,0:T(8,128)(2,1)} %k_ref.5, bf16[64,4096]{1,0:T(8,128)(2,1)} %v_ref.5, bf16[64,4096]{1,0:T(8,128)(2,1)} %g_ref.5), custom_call_target="tpu_custom_call" | custom-call | bytes 2097152 | tf_op jit(solution)/shard_map/own_half/pallas_call | solution.py:58
  11.9 1.0 collective-permute-done.other_ref
  12.9 0.0 copy-start.2
  12.9 1.5 %chunk_states.1 = bf16[32,2,64,128]{3,2,1,0:T(8,128)(2,1)} custom-call(bf16[4,64,2048]{2,1,0:T(8,128)(2,1)S(1)} %own_half.1.own_ref, bf16[4,64,2048]{2,1,0:T(8,128)(2,1)S(1)} %collective-permute-done.other_ref), custom_call_target="tpu_custom_call" | custom-call | tf_op jit(solution)/shard_map/chunk_states/pallas_call | solution.py:106
  14.4 3.9 %all-to-all-start = ((bf16[32,2,64,128]{3,2,1,0:T(8,128)(2,1)}), bf16[32,2,64,128]{3,2,1,0:T(8,128)(2,1)S(1)}, u32[]{:S(2)}, u32[]{:S(2)}) async-start(bf16[32,2,64,128]{3,2,1,0:T(8,128)(2,1)} %chunk_states.1), calls=%async_computation | async-start | bytes 2097152 | tf_op jit(solution)/shard_map/all_to_all | solution.py:349
  18.3 0.0 copy-done.2
  18.4 6.5 %inner_part.1 = (f32[3,128,2048]{2,1,0:T(8,128)}, bf16[3,128,2048]{2,1,0:T(8,128)(2,1)}) custom-call(s32[1]{0:T(128)} %bitcast.core_ref, bf16[64,4096]{1,0:T(8,128)(2,1)} %q_ref.5, bf16[64,4096]{1,0:T(8,128)(2,1)} %k_ref.5, bf16[64,4096]{1,0:T(8,128)(2,1)} %v_ref.5, bf16[64,4096]{1,0:T(8,128)(2,1)} %g_ref.5, bf16[4,64,2048]{2,1,0:T(8,128)(2,1)} %copy-done.2), custom_call_target="tpu_custom_call" | custom-call | flops 335544320 | bytes 12582912 | tf_op jit(solution)/shard_map/inner_part/pallas_call | solution.py:246
  24.9 10.1 %all-to-all-done.near_ref = bf16[32,2,64,128]{3,2,1,0:T(8,128)(2,1)S(1)} async-done(((bf16[32,2,64,128]{3,2,1,0:T(8,128)(2,1)}), bf16[32,2,64,128]{3,2,1,0:T(8,128)(2,1)S(1)}, u32[]{:S(2)}, u32[]{:S(2)}) %all-to-all-start) | async-done | bytes 1048608 | tf_op jit(solution)/shard_map/all_to_all | solution.py:349
  34.9 0.0 copy-start
  34.9 0.0 copy-start.1
  34.9 0.1 group_total.1
  35.1 24.7 %all_to_all.20.far_ref = bf16[8,4,16,128]{3,2,1,0:T(8,128)(2,1)S(1)} all-to-all(bf16[8,4,16,128]{3,2,1,0:T(8,128)(2,1)S(1)} %group_total.1), channel_id=1, replica_groups=mesh['yf'=1,'yh'=2,'yl'=2,'za'=2,'zb'=2,'zc'=2,'zl'=2,'x'=4,'core'=2] {'..., dimensions={0} | all-to-all | bytes 262144 | tf_op jit(solution)/shard_map/all_to_all | solution.py:349
  59.8 15.8 %all_to_all.21.carry_ref = bf16[8,4,16,128]{3,2,1,0:T(8,128)(2,1)S(1)} all-to-all(bf16[8,4,16,128]{3,2,1,0:T(8,128)(2,1)S(1)} %group_carry.1), channel_id=1, replica_groups=mesh['yf'=1,'yh'=2,'yl'=2,'za'=2,'zb'=2,'zc'=2,'zl'=2,'x'=4,'core'=2] {'..., dimensions={0} | all-to-all | bytes 262144 | tf_op jit(solution)/shard_map/all_to_all | solution.py:349
  75.6 0.2 chip_carry.1
  75.8 18.8 %all_to_all.22.carry_ref = bf16[32,2,64,128]{3,2,1,0:T(8,128)(2,1)S(1)} all-to-all(bf16[32,2,64,128]{3,2,1,0:T(8,128)(2,1)S(1)} %chip_carry.1), channel_id=1, replica_groups=mesh['yf'=1,'yh'=2,'yl'=2,'za'=2,'zb'=2,'zc'=2,'zl'=2,'x'=4,'core'=2] {'..., dimensions={0} | all-to-all | bytes 2097152 | tf_op jit(solution)/shard_map/all_to_all | solution.py:349
  94.6 0.0 copy-done
  94.6 0.0 copy-done.1
  94.6 0.9 other_gradients.1
  95.5 7.0 %collective-permute-start.1 = (bf16[3,64,2048]{2,1,0:T(8,128)(2,1)S(1)}, bf16[3,64,2048]{2,1,0:T(8,128)(2,1)S(1)}, u32[]{:S(2)}, u32[]{:S(2)}) collective-permute-start(bf16[3,64,2048]{2,1,0:T(8,128)(2,1)S(1)} %other_gradients.1), channel_id=1, source_target_pairs={{0,1},{1,0},{2,3},{3,2},{4,5},{5,4},{6,7},{7,6},{8,9},{9,8},{10,11... | collective-permute-start | bytes 2359304 | tf_op jit(solution)/shard_map/ppermute | solution.py:362
  102.6 1.7 %own_gradients.1 = (bf16[64,4096]{1,0:T(8,128)(2,1)}, bf16[64,4096]{1,0:T(8,128)(2,1)}, bf16[64,4096]{1,0:T(8,128)(2,1)}) custom-call(f32[3,128,2048]{2,1,0:T(8,128)S(1)} %copy-done, bf16[3,128,2048]{2,1,0:T(8,128)(2,1)S(1)} %copy-done.1, bf16[32,2,64,128]{3,2,1,0:T(8,128)(2,1)S(1)} %all_to_all.22.carry_ref), custom_call_target="tpu_custom_call" | custom-call | flops 100663296 | bytes 4194304 | tf_op jit(solution)/shard_map/own_gradients/pallas_call | solution.py:314
  104.3 0.2 collective-permute-done.1.got_ref
  104.5 0.9 place_half.1
  (1 shorter events, 0.0 us)
Async XLA Ops:
  1.9 11.1 %collective-permute-start = (bf16[4,64,2048]{2,1,0:T(8,128)(2,1)S(1)}, bf16[4,64,2048]{2,1,0:T(8,128)(2,1)S(1)}, u32[]{:S(2)}, u32[]{:S(2)}) collective-permute-start(bf16[4,64,2048]{2,1,0:T(8,128)(2,1)S(1)} %other_half.1), channel_id=1, source_target_pairs={{0,1},{1,0},{2,3},{3,2},{4,5},{5,4},{6,7},{7,6},{8,9},{9,8},{10,11... | collective-permute-start | bytes 3145736 | tf_op jit(solution)/shard_map/ppermute | solution.py:356
  12.9 5.4 %copy-start.2 = (bf16[4,64,2048]{2,1,0:T(8,128)(2,1)}, bf16[4,64,2048]{2,1,0:T(8,128)(2,1)S(1)}, u32[]{:S(2)}) copy-start(bf16[4,64,2048]{2,1,0:T(8,128)(2,1)S(1)} %collective-permute-done.other_ref) | copy-start | bytes 3145732
  14.4 20.5 %all-to-all-start = ((bf16[32,2,64,128]{3,2,1,0:T(8,128)(2,1)}), bf16[32,2,64,128]{3,2,1,0:T(8,128)(2,1)S(1)}, u32[]{:S(2)}, u32[]{:S(2)}) async-start(bf16[32,2,64,128]{3,2,1,0:T(8,128)(2,1)} %chunk_states.1), calls=%async_computation | async-start | bytes 2097152 | tf_op jit(solution)/shard_map/all_to_all | solution.py:349
  34.9 59.7 %copy-start = (f32[3,128,2048]{2,1,0:T(8,128)S(1)}, f32[3,128,2048]{2,1,0:T(8,128)}, u32[]{:S(2)}) copy-start(f32[3,128,2048]{2,1,0:T(8,128)} %get-tuple-element.13.inner_ref) | copy-start | bytes 9437188
  34.9 59.7 %copy-start.1 = (bf16[3,128,2048]{2,1,0:T(8,128)(2,1)S(1)}, bf16[3,128,2048]{2,1,0:T(8,128)(2,1)}, u32[]{:S(2)}) copy-start(bf16[3,128,2048]{2,1,0:T(8,128)(2,1)} %get-tuple-element.14.kept_ref) | copy-start | bytes 4718596
  95.5 8.9 %collective-permute-start.1 = (bf16[3,64,2048]{2,1,0:T(8,128)(2,1)S(1)}, bf16[3,64,2048]{2,1,0:T(8,128)(2,1)S(1)}, u32[]{:S(2)}, u32[]{:S(2)}) collective-permute-start(bf16[3,64,2048]{2,1,0:T(8,128)(2,1)S(1)} %other_gradients.1), channel_id=1, source_target_pairs={{0,1},{1,0},{2,3},{3,2},{4,5},{5,4},{6,7},{7,6},{8,9},{9,8},{10,11... | collective-permute-start | bytes 2359304 | tf_op jit(solution)/shard_map/ppermute | solution.py:362
